TPU v7x, 512 devices: a whole 4x8x8 slice. The times are simulated.
512 devices in a mesh: mem: 64 (over x, y, core), patch: 8 (over z).
Axes of the slice: x: 4, y: 8, z: 8, core: 2. Of those that a mesh axis runs over, the one named last changes fastest.
Arguments:
- state: bfloat16 [3, 1024, 131072], P(None, 'mem', 'patch'), may hold values from -6 to 6
- obs_noise: bfloat16 [1024, 131072], P('mem', 'patch'), may hold values from -6 to 6
- obs_values: float32 [8, 16384], P('patch', 'mem'), may hold values from -6 to 6
- obs_weights: bfloat16 [8, 128, 128, 128], P('patch', 'mem'), may hold values from -1 to 1
- tapers: float32 [8, 128, 128], replicated, may hold values from 0.2 to 1
- pair_source: int32 [8, 128, 4], P('patch', 'mem'), may hold values from 0 to 127, as said below
- pair_taper: int32 [8, 128, 4], P('patch', 'mem'), may hold values from 0 to 7
Outputs:
- analysis: bfloat16 [3, 1024, 131072], P(None, 'mem', 'patch')
Inputs may be any that keep to these rules, and one draw needn't show every extreme that they name: `pair_source`: each listed source lies in the same patch within 2 blocks of its target block; positions beyond the patch's ends are moved to its first or last block.
All inputs are finite; a program needn't handle non-finite values.
Results may differ from a plain program's by a relative error of at most 0.0058.
Values may be sent and summed in bfloat16 or wider, within the bound.
No kernel may reach another device: no remote copies, remote signals or barrier semaphores. Data moves between devices by JAX's collectives and lax.ppermute only.
A program may use at most 64 MiB of HBM per device.

v0:
```python
import jax
import jax.numpy as jnp
from jax import lax
from jax.sharding import PartitionSpec as P

MEMBERS = 1024
VARIABLES = 3
BLOCK_CELLS = 128
RADIUS = 2
PAIRS = 4
BLOCKS_DEV = 2


def padded(cells, sides, width):
    for axis, dim in sides:
        count = lax.axis_size(axis)
        ends = count - 1
        head = lax.slice_in_dim(cells, 0, width, axis=dim)
        tail = lax.slice_in_dim(cells, cells.shape[dim] - width, cells.shape[dim], axis=dim)
        cells = jnp.concatenate(
            [
                lax.ppermute(tail, axis, [(i, (i + 1) % count) for i in range(ends)]),
                cells,
                lax.ppermute(head, axis, [((i + 1) % count, i) for i in range(ends)]),
            ],
            axis=dim,
        )
    return cells


def centered(values):
    wide = values.astype(jnp.float32)
    return (wide - jnp.mean(wide, axis=-2, keepdims=True)).astype(jnp.bfloat16)


def on_device(state, obs_noise, obs_values, obs_weights, tapers, pair_source, pair_taper):
    columns = lax.all_to_all(state, "mem", split_axis=2, concat_axis=1, tiled=True)
    noise_cols = lax.all_to_all(obs_noise, "mem", split_axis=1, concat_axis=0, tiled=True)
    observed = columns[0]
    members = observed.shape[0]
    owned = observed.shape[1]
    anom_first = centered(observed)
    innovation = (
        obs_values[0][None, :] + noise_cols.astype(jnp.float32) - observed.astype(jnp.float32)
    ).astype(jnp.bfloat16)
    weighted = jnp.einsum(
        "nkd,kcd->nkc",
        innovation.reshape(members, BLOCKS_DEV, BLOCK_CELLS),
        obs_weights[0],
        preferred_element_type=jnp.float32,
    )
    weighted = weighted.astype(jnp.bfloat16).reshape(members, owned)
    window = padded(jnp.stack([anom_first, weighted]), (("mem", 2),), RADIUS * BLOCK_CELLS)
    anomalies = centered(columns)
    first_block = lax.axis_index("mem") * BLOCKS_DEV
    results = []
    for block in range(BLOCKS_DEV):
        target_anom = anomalies[:, :, block * BLOCK_CELLS : (block + 1) * BLOCK_CELLS]
        slices = []
        taper_tiles = []
        for slot in range(PAIRS):
            offset = (pair_source[0, block, slot] - first_block + RADIUS) * BLOCK_CELLS
            slices.append(lax.dynamic_slice_in_dim(window, offset, BLOCK_CELLS, 2))
            taper_tiles.append(
                lax.dynamic_index_in_dim(tapers, pair_taper[0, block, slot], 0, keepdims=False)
            )
        sources = jnp.concatenate(slices, axis=2)
        taper_row = jnp.concatenate(taper_tiles, axis=1)
        pieces = []
        for variable in range(VARIABLES):
            covariance = lax.dot_general(
                target_anom[variable],
                sources[0],
                (((0,), (0,)), ((), ())),
                preferred_element_type=jnp.float32,
            ) / (MEMBERS - 1)
            localized = (taper_row * covariance).astype(jnp.bfloat16)
            pieces.append(
                lax.dot_general(
                    sources[1],
                    localized,
                    (((1,), (1,)), ((), ())),
                    preferred_element_type=jnp.float32,
                )
            )
        total = jnp.stack(pieces)
        results.append(total)
    increment = jnp.concatenate(results, axis=2)
    updated = (columns.astype(jnp.float32) + increment).astype(jnp.bfloat16)
    return lax.all_to_all(updated, "mem", split_axis=1, concat_axis=2, tiled=True)


def solution(mesh):
    placed = (
        P(None, "mem", "patch"),
        P("mem", "patch"),
        P("patch", "mem"),
        P("patch", "mem", None, None),
        P(),
        P("patch", "mem", None),
        P("patch", "mem", None),
    )
    return jax.shard_map(
        on_device, mesh=mesh, in_specs=placed, out_specs=P(None, "mem", "patch"), check_vma=False
    )
```

profile of v0, /device:TPU:1, one launch (start us, length us, event | category | flops | bytes accessed | tf_op | source)
XLA Modules:
  0.0 259.1 jit_solution(17874046500938926867)
XLA Ops:
  0.0 0.0 copy-start
  0.0 2.0 copy.42
  2.0 11.6 %all-to-all-start.1 = ((bf16[16,64,256]{2,0,1:T(8,128)(2,1)}), bf16[16,64,256]{2,0,1:T(8,128)(2,1)S(1)}, u32[]{:S(2)}, u32[]{:S(2)}) async-start(bf16[16,64,256]{2,0,1:T(8,128)(2,1)} %bitcast.125), calls=%async_computation.1 | async-start | bytes 1048576 | tf_op jit(solution)/shard_map/all_to_all | solution.py:38
  13.6 0.0 copy-done.9
  13.7 15.7 %copy.24 = bf16[3,16,16384]{1,0,2:T(4,128)(2,1)} copy(bf16[3,16,16384]{2,1,0:T(8,128)(2,1)S(1)} %copy-done.9) | data formatting | bytes 3145728 | tf_op args[0]
  29.4 26.2 %reshape.70 = bf16[64,2,6144]{2,1,0:T(2,128)(2,1)} reshape(bf16[16384,3,16]{2,1,0:T(4,128)(2,1)} %bitcast.127) | data formatting | bytes 3145728
  55.6 0.0 all-to-all-done.1
  55.6 10.5 %all-to-all-start = ((bf16[64,2,6144]{2,1,0:T(2,128)(2,1)}), bf16[64,2,6144]{2,1,0:T(2,128)(2,1)S(1)}, u32[]{:S(2)}, u32[]{:S(2)}) async-start(bf16[64,2,6144]{2,1,0:T(2,128)(2,1)} %reshape.70), calls=%async_computation | async-start | bytes 3145728 | tf_op jit(solution)/shard_map/all_to_all | solution.py:37
  66.1 0.0 copy-done.14
  66.1 0.7 fusion.36
  71.9 0.0 copy-done.15
  71.9 0.7 fusion.35
  88.1 0.0 copy-done.10
  88.1 0.7 dynamic-slice_bitcast_fusion.7
  88.8 0.1 convert_bitcast_fusion
  88.9 1.5 reshape.68
  90.4 15.4 %all-to-all-done = bf16[64,2,6144]{2,1,0:T(2,128)(2,1)S(1)} async-done(((bf16[64,2,6144]{2,1,0:T(2,128)(2,1)}), bf16[64,2,6144]{2,1,0:T(2,128)(2,1)S(1)}, u32[]{:S(2)}, u32[]{:S(2)}) %all-to-all-start) | async-done | bytes 1572896 | tf_op jit(solution)/shard_map/all_to_all | solution.py:37
  105.9 21.0 %reshape.71 = bf16[16384,3,16]{2,1,0:T(4,128)(2,1)} reshape(bf16[64,2,6144]{2,1,0:T(2,128)(2,1)S(1)} %all-to-all-done) | data formatting | bytes 3145728
  126.9 15.3 %copy.36 = bf16[3,16,64,256]{3,2,1,0:T(8,128)(2,1)S(1)} copy(bf16[3,16,64,256]{1,0,3,2:T(4,128)(2,1)} %bitcast.126) | data formatting | bytes 3145728 | tf_op jit(solution)/shard_map/all_to_all | solution.py:37
  142.1 0.0 copy-start.2
  142.2 0.1 slice_convert_fusion
  142.3 0.2 fusion.15
  142.4 0.6 copy.27
  143.0 1.5 reshape.69
  144.6 0.0 copy-done.16
  144.6 2.1 subtract_convert_fusion.1
  146.6 0.0 copy-done
  146.7 1.1 convolution_convert_fusion
  147.8 1.2 copy.31
  149.0 0.0 copy-start.4
  149.0 0.1 fusion.13
  149.1 0.0 copy-start.6
  149.1 1.2 pad_maximum_fusion.3
  150.4 2.1 collective-permute-start.1
  152.5 0.0 copy-done.6
  152.5 3.7 %collective-permute-start = (bf16[2,1024,256]{2,1,0:T(8,128)(2,1)}, bf16[2,1024,256]{2,1,0:T(8,128)(2,1)}, u32[]{:S(2)}, u32[]{:S(2)}) collective-permute-start(bf16[2,1024,256]{2,1,0:T(8,128)(2,1)} %pad_maximum_fusion.3), channel_id=1, source_target_pairs={{0,8},{8,16},{16,24},{24,32},{32,40},{40,48},{48,56},{56,64},{64,7... | collective-permute-start | bytes 3145736 | tf_op jit(solution)/shard_map/ppermute | solution.py:22
  156.1 0.0 copy-done.2
  156.2 0.0 copy-done.4
  156.2 0.4 bitcast_convert_fusion
  156.6 1.8 copy.26
  158.4 2.3 copy.32
  160.7 1.7 convert_reduce_fusion
  162.4 0.0 copy-start.5
  162.5 1.4 subtract_convert_fusion
  163.9 2.9 %collective-permute-done.1 = bf16[2,1024,256]{2,1,0:T(8,128)(2,1)} collective-permute-done((bf16[2,1024,256]{2,1,0:T(8,128)(2,1)}, bf16[2,1024,256]{2,1,0:T(8,128)(2,1)}, u32[]{:S(2)}, u32[]{:S(2)}) %collective-permute-start.1) | collective-permute-done | bytes 1048608 | tf_op jit(solution)/shard_map/ppermute | solution.py:24
  166.8 1.2 collective-permute-done
  168.0 1.6 pad_maximum_fusion
  169.7 0.9 constant_dynamic-slice_fusion.7
  170.5 0.0 copy-start.11
  170.6 0.0 copy-start.12
  170.6 0.0 copy-start.13
  170.6 1.6 pad_maximum_fusion.1
  172.2 0.0 copy-done.12
  172.2 3.9 %convolution_bitcast_fusion = f32[1,1024,128]{1,2,0:T(8,128)} fusion(bf16[2,1024,512]{2,1,0:T(8,128)(2,1)} %get-tuple-element.38, bf16[3,1024,256]{2,1,0:T(8,128)(2,1)} %subtract_convert_fusion, f32[128,128]{1,0:T(8,128)S(1)} %copy-done.12, f32[128,128]{1,0:T(8,128)S(1)} %copy-done.13, f32[128,128]{1,0:T(8,128)S(1)} %get-tuple-element.14, ...), kind=kOutput, calls=%fused_computation.7 | convolution fusion | flops 268828672 | bytes 3145728 | tf_op jit(solution)/shard_map/dot_general | solution.py:79
  176.1 3.2 %convolution_bitcast_fusion.1 = f32[1,1024,128]{1,2,0:T(8,128)} fusion(bf16[2,1024,512]{2,1,0:T(8,128)(2,1)} %get-tuple-element.38, bf16[3,1024,256]{2,1,0:T(8,128)(2,1)} %subtract_convert_fusion, f32[128,128]{1,0:T(8,128)S(1)} %copy-done.12, f32[128,128]{1,0:T(8,128)S(1)} %copy-done.13, f32[128,128]{1,0:T(8,128)S(1)} %get-tuple-element.14, ...), kind=kOutput, calls=%fused_computation.8 | convolution fusion | flops 268828672 | bytes 3145728 | tf_op jit(solution)/shard_map/dot_general | solution.py:79
  179.3 3.2 %convolution_bitcast_fusion.2 = f32[1,1024,128]{1,2,0:T(8,128)} fusion(bf16[2,1024,512]{2,1,0:T(8,128)(2,1)} %get-tuple-element.38, bf16[3,1024,256]{2,1,0:T(8,128)(2,1)} %subtract_convert_fusion, f32[128,128]{1,0:T(8,128)S(1)} %copy-done.12, f32[128,128]{1,0:T(8,128)S(1)} %copy-done.13, f32[128,128]{1,0:T(8,128)S(1)} %get-tuple-element.14, ...), kind=kOutput, calls=%fused_computation.9 | convolution fusion | flops 268828672 | bytes 3145728 | tf_op jit(solution)/shard_map/dot_general | solution.py:79
  182.5 2.5 convolution_bitcast_fusion.3
  184.9 2.5 convolution_bitcast_fusion.4
  187.4 3.3 %convolution_bitcast_fusion.5 = f32[1,1024,128]{1,2,0:T(8,128)} fusion(bf16[2,1024,512]{2,1,0:T(8,128)(2,1)} %copy-done.8, bf16[3,1024,256]{2,1,0:T(8,128)(2,1)} %subtract_convert_fusion, f32[128,128]{1,0:T(8,128)S(1)} %get-tuple-element.16, f32[128,128]{1,0:T(8,128)S(1)} %get-tuple-element.17, f32[128,128]{1,0:T(8,128)S(1)} %get-tuple-element.18, ...), kind=kOutput, calls=%fused_computation.12 | convolution fusion | flops 268828672 | bytes 3145728 | tf_op jit(solution)/shard_map/dot_general | solution.py:79
  190.7 3.5 %fusion = bf16[3,1024,256]{1,2,0:T(8,128)(2,1)} fusion(f32[3,1024,256]{1,2,0:T(8,128)S(1)} %copy-done.3, f32[1,1024,128]{1,2,0:T(8,128)} %convolution_bitcast_fusion, f32[1,1024,128]{1,2,0:T(8,128)} %convolution_bitcast_fusion.1, f32[1,1024,128]{1,2,0:T(8,128)} %convolution_bitcast_fusion.2, f32[1,1024,128]{1,2,0:T(8,128)} %convolution_bitcast_fusion.3, ...), kind=kLoop, calls=%fused_computation.2 | loop fusion | flops 5505024 | bytes 7864320 | tf_op jit(solution)/shard_map/convert_element_type | solution.py:89
  194.2 2.9 %copy.33 = bf16[3,1024,256]{2,0,1:T(4,128)(2,1)S(1)} copy(bf16[3,1024,256]{1,2,0:T(8,128)(2,1)} %fusion) | data formatting | bytes 3145728 | tf_op jit(solution)/shard_map/convert_element_type | solution.py:89
  197.1 60.5 %all_to_all.46 = bf16[3,1024,256]{2,0,1:T(4,128)(2,1)S(1)} all-to-all(bf16[3,1024,256]{2,0,1:T(4,128)(2,1)S(1)} %copy.33), channel_id=1, replica_groups=mesh['mem'=64,'patch'=8] {'mem'}, dimensions={1} | all-to-all | bytes 3145728 | tf_op jit(solution)/shard_map/all_to_all | solution.py:90
  257.6 0.2 copy.34
  257.8 1.2 copy.38
  (18 shorter events, 0.0 us)
Async XLA Ops:
  0.0 146.6 %copy-start = (bf16[1,2,128,128]{3,2,1,0:T(8,128)(2,1)S(1)}, bf16[1,2,128,128]{3,2,1,0:T(8,128)(2,1)}, u32[]{:S(2)}) copy-start(bf16[1,2,128,128]{3,2,1,0:T(8,128)(2,1)} %param.10) | copy-start | bytes 196612
  0.0 13.6 %copy-start.9 = (bf16[3,16,16384]{2,1,0:T(8,128)(2,1)S(1)}, bf16[3,16,16384]{2,1,0:T(8,128)(2,1)}, u32[]{:S(2)}) copy-start(bf16[3,16,16384]{2,1,0:T(8,128)(2,1)} %param.7) | copy-start | bytes 4718596
  2.0 53.6 %all-to-all-start.1 = ((bf16[16,64,256]{2,0,1:T(8,128)(2,1)}), bf16[16,64,256]{2,0,1:T(8,128)(2,1)S(1)}, u32[]{:S(2)}, u32[]{:S(2)}) async-start(bf16[16,64,256]{2,0,1:T(8,128)(2,1)} %bitcast.125), calls=%async_computation.1 | async-start | bytes 1048576 | tf_op jit(solution)/shard_map/all_to_all | solution.py:38
  55.6 10.5 %copy-start.14 = (s32[1,2,4]{2,1,0:T(2,128)S(1)}, s32[1,2,4]{2,1,0:T(2,128)}, u32[]{:S(2)}) copy-start(s32[1,2,4]{2,1,0:T(2,128)} %param.12) | copy-start | bytes 100
  55.6 16.4 %copy-start.15 = (s32[1,2,4]{2,1,0:T(2,128)S(1)}, s32[1,2,4]{2,1,0:T(2,128)}, u32[]{:S(2)}) copy-start(s32[1,2,4]{2,1,0:T(2,128)} %param.13) | copy-start | bytes 100
  55.6 32.5 %copy-start.10 = (f32[8,128,128]{2,1,0:T(8,128)S(1)}, f32[8,128,128]{2,1,0:T(8,128)}, u32[]{:S(2)}) copy-start(f32[8,128,128]{2,1,0:T(8,128)} %param.11) | copy-start | bytes 1572868
  55.6 50.3 %all-to-all-start = ((bf16[64,2,6144]{2,1,0:T(2,128)(2,1)}), bf16[64,2,6144]{2,1,0:T(2,128)(2,1)S(1)}, u32[]{:S(2)}, u32[]{:S(2)}) async-start(bf16[64,2,6144]{2,1,0:T(2,128)(2,1)} %reshape.70), calls=%async_computation | async-start | bytes 3145728 | tf_op jit(solution)/shard_map/all_to_all | solution.py:37
  142.1 14.0 %copy-start.2 = (bf16[3,16,64,256]{3,2,1,0:T(8,128)(2,1)}, bf16[3,16,64,256]{3,2,1,0:T(8,128)(2,1)S(1)}, u32[]{:S(2)}) copy-start(bf16[3,16,64,256]{3,2,1,0:T(8,128)(2,1)S(1)} %copy.36) | copy-start | bytes 4718596
  142.4 2.1 copy-start.16
  149.0 7.1 %copy-start.4 = (bf16[1,1024,256]{2,1,0:T(8,128)(2,1)}, bf16[1,1024,256]{2,1,0:T(8,128)(2,1)S(1)}, u32[]{:S(2)}) copy-start(bf16[1,1024,256]{2,1,0:T(8,128)(2,1)S(1)} %copy.31) | copy-start | bytes 1572868
  149.1 3.3 %copy-start.6 = (bf16[1,1024,256]{2,1,0:T(8,128)(2,1)}, bf16[1,1024,256]{2,1,0:T(8,128)(2,1)S(1)}, u32[]{:S(2)}) copy-start(bf16[1,1024,256]{2,1,0:T(8,128)(2,1)S(1)} %fusion.13) | copy-start | bytes 1572868
  150.4 16.4 %collective-permute-start.1 = (bf16[2,1024,256]{2,1,0:T(8,128)(2,1)}, bf16[2,1024,256]{2,1,0:T(8,128)(2,1)}, u32[]{:S(2)}, u32[]{:S(2)}) collective-permute-start(bf16[2,1024,256]{2,1,0:T(8,128)(2,1)} %pad_maximum_fusion.3), channel_id=1, source_target_pairs={{8,0},{16,8},{24,16},{32,24},{40,32},{48,40},{56,48},{64,56},{72,6... | collective-permute-start | bytes 3145736 | tf_op jit(solution)/shard_map/ppermute | solution.py:24
  152.5 15.5 %collective-permute-start = (bf16[2,1024,256]{2,1,0:T(8,128)(2,1)}, bf16[2,1024,256]{2,1,0:T(8,128)(2,1)}, u32[]{:S(2)}, u32[]{:S(2)}) collective-permute-start(bf16[2,1024,256]{2,1,0:T(8,128)(2,1)} %pad_maximum_fusion.3), channel_id=1, source_target_pairs={{0,8},{8,16},{16,24},{24,32},{32,40},{40,48},{48,56},{56,64},{64,7... | collective-permute-start | bytes 3145736 | tf_op jit(solution)/shard_map/ppermute | solution.py:22
  162.4 5.6 %copy-start.5 = (bf16[1,1024,256]{2,1,0:T(8,128)(2,1)S(1)}, bf16[1,1024,256]{2,1,0:T(8,128)(2,1)}, u32[]{:S(2)}) copy-start(bf16[1,1024,256]{2,1,0:T(8,128)(2,1)} %copy-done.4) | copy-start | bytes 1572868
  162.5 5.6 %copy-start.7 = (bf16[1,1024,256]{2,1,0:T(8,128)(2,1)S(1)}, bf16[1,1024,256]{2,1,0:T(8,128)(2,1)}, u32[]{:S(2)}) copy-start(bf16[1,1024,256]{2,1,0:T(8,128)(2,1)} %copy-done.6) | copy-start | bytes 1572868
  170.5 1.6 copy-start.11
  170.6 1.6 copy-start.12
  170.6 1.6 copy-start.13
  172.2 12.8 %copy-start.8 = (bf16[2,1024,512]{2,1,0:T(8,128)(2,1)}, bf16[2,1024,512]{2,1,0:T(8,128)(2,1)S(1)}, u32[]{:S(2)}) copy-start(bf16[2,1024,512]{2,1,0:T(8,128)(2,1)S(1)} %get-tuple-element.37) | copy-start | bytes 6291460
  187.4 3.3 %copy-start.3 = (f32[3,1024,256]{1,2,0:T(8,128)S(1)}, f32[3,1024,256]{1,2,0:T(8,128)}, u32[]{:S(2)}) copy-start(f32[3,1024,256]{1,2,0:T(8,128)} %copy.32) | copy-start | bytes 9437188
  257.6 1.5 copy-start.1
where the time goes:
time: 261 us; the launch traced here: 259 us
  local copies, waits for them, and re-layouts  96.7 us (37%)
  blocking collectives  60.5 us (23%)
  starting transfers between devices  27.8 us (11%)
  between operations  20.9 us (8%)
  matrix products  19.6 us (8%)
  waiting for transfers between devices  19.5 us (7%)
  other arithmetic  14 us (5%)
    unnamed x37, local copies, waits for them, and re-layouts  63 us
    all_to_all x1, blocking collectives, on_device(): lax.all_to_all(updated, 'mem', split_axis=1, concat_axis=2, tiled=True)  60.5 us
    dot_general x6, matrix products, on_device(): lax.dot_general(sources[1], localized, (((1,), (1,)), ((), ())), preferre...  18.5 us
    all_to_all x1, waiting for transfers between devices, on_device(): lax.all_to_all(state, 'mem', split_axis=2, concat_axis=1, tiled=True)  15.4 us
    all_to_all x1, local copies, waits for them, and re-layouts, on_device(): lax.all_to_all(state, 'mem', split_axis=2, concat_axis=1, tiled=True)  15.3 us
    all_to_all x1, starting transfers between devices, on_device(): lax.all_to_all(obs_noise, 'mem', split_axis=1, concat_axis=0, tiled=True)  11.6 us
    all_to_all x1, starting transfers between devices, on_device(): lax.all_to_all(state, 'mem', split_axis=2, concat_axis=1, tiled=True)  10.5 us
    convert_element_type x3, local copies, waits for them, and re-layouts, on_device(): updated = (columns.astype(jnp.float32) + increment).astype(jnp.bfloat16)  7.09 us
  transfers between devices with their start and end apart: 4, of which 3 were waited for; matrix products, arithmetic and copies ran while one was open for 21% of the time, Pallas kernels for 0%

commit v1 on v0

v1 whole, which is shorter than its diff:
```python
import jax
import jax.numpy as jnp
from jax import lax
from jax.experimental import pallas as pl
from jax.experimental.pallas import tpu as pltpu
from jax.sharding import PartitionSpec as P

MEMBERS = 1024
VARIABLES = 3
BLOCK = 128
RADIUS = 2
PAIRS = 4
OWNED = 2
CELLS = OWNED * BLOCK
LOCAL_MEMBERS = 16
RING = 64
TILES = MEMBERS // BLOCK

VMEM = pl.BlockSpec(memory_space=pltpu.VMEM)
SMEM = pl.BlockSpec(memory_space=pltpu.SMEM)
PARAMS = pltpu.CompilerParams(vmem_limit_bytes=40 * 1024 * 1024)
BF16 = jnp.bfloat16
F32 = jnp.float32


def shape(*dims, dtype=BF16):
    return jax.ShapeDtypeStruct(dims, dtype)


def columns(ref, slot):
    return ref[:, slot].reshape(MEMBERS, CELLS)


def prepare_kernel(arrived, obs, weights, edges):
    first = columns(arrived, 0).astype(F32)
    noise = columns(arrived, 1).astype(F32)
    mean = jnp.sum(first, axis=0, keepdims=True) * (1.0 / MEMBERS)
    anomaly = (first - mean).astype(BF16)
    innovation = (obs[...] + noise - first).astype(BF16)
    for block in range(OWNED):
        lanes = slice(block * BLOCK, (block + 1) * BLOCK)
        edges[1, block] = lax.dot_general(
            innovation[:, lanes],
            weights[block],
            (((1,), (1,)), ((), ())),
            preferred_element_type=F32,
        ).astype(BF16)
        for tile in range(TILES):
            rows = slice(tile * BLOCK, (tile + 1) * BLOCK)
            edges[0, block, rows] = anomaly[rows, lanes].T


def source_rows(window, source):
    tiles = [window[0, source, tile * BLOCK : (tile + 1) * BLOCK] for tile in range(TILES)]
    return jnp.concatenate(tiles, axis=1)


def block_update(window, sums, tapers, index, block, values, count):
    wide, raw = values
    mean = jnp.sum(wide, axis=0, keepdims=True) * (1.0 / MEMBERS)
    sources = [index[block, pair] for pair in range(PAIRS)]
    left = jnp.concatenate([source_rows(window, s) for s in sources], axis=0)
    covariance = jnp.dot(left, raw, preferred_element_type=F32)
    pieces = []
    for pair in range(PAIRS):
        part = covariance[pair * BLOCK : (pair + 1) * BLOCK]
        part = part - sums[sources[pair]][:, :1] * mean
        taper = tapers[block, pair]
        pieces.append((part * jnp.concatenate([taper] * count, axis=1)).astype(BF16))
    localized = jnp.concatenate(pieces, axis=0)
    weighted = jnp.concatenate([window[1, s] for s in sources], axis=1)
    return wide + jnp.dot(weighted, localized, preferred_element_type=F32)


def first_kernel(index, taper_at, before, middle, after, arrived, table, window, sums, tapers, out):
    for place, part in enumerate((before, middle, after)):
        for kind in range(2):
            window[kind, place * OWNED : (place + 1) * OWNED] = part[kind]
    for source in range(3 * OWNED):
        total = jnp.sum(source_rows(window, source).astype(F32), axis=1, keepdims=True)
        sums[source] = jnp.broadcast_to(total, (BLOCK, BLOCK))
    for block in range(OWNED):
        for pair in range(PAIRS):
            tapers[block, pair] = table[taper_at[block, pair]].T * (1.0 / (MEMBERS - 1))
    for block in range(OWNED):
        lanes = slice(block * BLOCK, (block + 1) * BLOCK)
        raw = arrived[:, 0, :, lanes].reshape(MEMBERS, BLOCK)
        result = block_update(window, sums, tapers, index, block, (raw.astype(F32), raw), 1)
        out[:, :, lanes] = result.astype(BF16).reshape(RING, LOCAL_MEMBERS, BLOCK)


def rest_kernel(index, window, sums, tapers, arrived, first, out):
    out[:, 0] = first[...]
    for block in range(OWNED):
        lanes = slice(block * BLOCK, (block + 1) * BLOCK)
        raw = jnp.concatenate(
            [arrived[:, v, :, lanes].reshape(MEMBERS, BLOCK) for v in range(2)], axis=1
        )
        result = block_update(window, sums, tapers, index, block, (raw.astype(F32), raw), 2)
        for v in range(2):
            part = result[:, v * BLOCK : (v + 1) * BLOCK].astype(BF16)
            out[:, 1 + v, :, lanes] = part.reshape(RING, LOCAL_MEMBERS, BLOCK)


def pack_kernel(*refs):
    sources, out = refs[:-1], refs[-1]
    for slot, ref in enumerate(sources):
        for owner in range(RING):
            out[owner, slot] = ref[:, owner * CELLS : (owner + 1) * CELLS]


def pack(*arrays):
    count = len(arrays)
    return pl.pallas_call(
        pack_kernel,
        out_shape=shape(RING, count, LOCAL_MEMBERS, CELLS),
        in_specs=[VMEM] * count,
        out_specs=VMEM,
        compiler_params=PARAMS,
    )(*arrays)


def exchange(packed):
    return lax.all_to_all(packed, "mem", split_axis=0, concat_axis=0, tiled=True)


def on_device(state, obs_noise, obs_values, obs_weights, tapers, pair_source, pair_taper):
    arrived = exchange(pack(state[0], obs_noise))
    others = exchange(pack(state[1], state[2]))
    edges = pl.pallas_call(
        prepare_kernel,
        out_shape=shape(2, OWNED, MEMBERS, BLOCK),
        in_specs=[VMEM] * 3,
        out_specs=VMEM,
        compiler_params=PARAMS,
    )(arrived, obs_values, obs_weights[0])
    ends = RING - 1
    before = lax.ppermute(edges, "mem", [(i, i + 1) for i in range(ends)])
    after = lax.ppermute(edges, "mem", [(i + 1, i) for i in range(ends)])
    index = pair_source[0] - (lax.axis_index("mem") * OWNED - RADIUS)
    window, sums, taper_tiles, first = pl.pallas_call(
        first_kernel,
        out_shape=(
            shape(2, 3 * OWNED, MEMBERS, BLOCK),
            shape(3 * OWNED, BLOCK, BLOCK, dtype=F32),
            shape(OWNED, PAIRS, BLOCK, BLOCK, dtype=F32),
            shape(RING, LOCAL_MEMBERS, CELLS),
        ),
        in_specs=[SMEM, SMEM] + [VMEM] * 5,
        out_specs=(VMEM,) * 4,
        compiler_params=PARAMS,
    )(index, pair_taper[0], before, edges, after, arrived, tapers)
    updated = pl.pallas_call(
        rest_kernel,
        out_shape=shape(RING, VARIABLES, LOCAL_MEMBERS, CELLS),
        in_specs=[SMEM] + [VMEM] * 5,
        out_specs=VMEM,
        compiler_params=PARAMS,
    )(index, window, sums, taper_tiles, others, first)
    back = exchange(updated)
    return jnp.transpose(back, (1, 2, 0, 3)).reshape(VARIABLES, LOCAL_MEMBERS, RING * CELLS)


def solution(mesh):
    placed = (
        P(None, "mem", "patch"),
        P("mem", "patch"),
        P("patch", "mem"),
        P("patch", "mem", None, None),
        P(),
        P("patch", "mem", None),
        P("patch", "mem", None),
    )
    return jax.shard_map(
        on_device, mesh=mesh, in_specs=placed, out_specs=P(None, "mem", "patch"), check_vma=False
    )
```

time: 261 us -> 150 us (0.57)
  local copies, waits for them, and re-layouts: 96.7 us -> 11 us
  waiting for transfers between devices: 19.5 us -> 57.4 us
  between operations: 20.9 us -> 0.14 us
  matrix products: 19.6 us -> 0 us
  other arithmetic: 14 us -> 0.01 us
  blocking collectives: 60.5 us -> 49.1 us
  Pallas kernels: 0 us -> 8.71 us
  starting transfers between devices: 27.8 us -> 23.4 us
    unnamed x37 -> x24, local copies, waits for them, and re-layouts: 63 us -> 8.25 us
    ppermute x2, waiting for transfers between devices: 4.11 us -> 29.9 us  [the longest x1 29.9 us: on_device(): after = lax.ppermute(edges, 'mem', [(i + 1, i) for i in range(ends)])]
    dot_general x7 -> x0, matrix products: 19.6 us -> none  [the longest x6 18.5 us: on_device(): lax.dot_general(sources[1], localized, (((1,), (1,)), ((), ())), preferre...]
    all_to_all x4 -> x0, local copies, waits for them, and re-layouts: 18.7 us -> none  [the longest x1 15.3 us: on_device(): lax.all_to_all(state, 'mem', split_axis=2, concat_axis=1, tiled=True)]
    all_to_all x2, waiting for transfers between devices: 15.4 us -> 27.5 us  [exchange(): lax.all_to_all(packed, 'mem', split_axis=0, concat_axis=0, tiled=True)]
    all_to_all x1, blocking collectives: 60.5 us -> 49.1 us  [exchange(): lax.all_to_all(packed, 'mem', split_axis=0, concat_axis=0, tiled=True)]
    convert_element_type x6 -> x0, local copies, waits for them, and re-layouts: 10.7 us -> none  [the longest x3 7.09 us: on_device(): updated = (columns.astype(jnp.float32) + increment).astype(jnp.bfloat16)]
    pallas_call x0 -> x5, Pallas kernels: none -> 8.71 us  [the longest x1 3.7 us: on_device(): pl.pallas_call(first_kernel, out_shape=(shape(2, 3 * OWNED, MEMBERS, BLOC...]
  transfers between devices with their start and end apart: 4 -> 4, of which waited for: 3 -> 2; matrix products, arithmetic and copies ran while one was open for 21% -> 0% of each run, Pallas kernels for 0% -> 3%
where the time goes in v1:
time: 150 us
  waiting for transfers between devices  57.4 us (38%)
  blocking collectives  49.1 us (33%)
  starting transfers between devices  23.4 us (16%)
  local copies, waits for them, and re-layouts  11 us (7%)
  Pallas kernels  8.71 us (6%)
    all_to_all x1, blocking collectives, exchange(): lax.all_to_all(packed, 'mem', split_axis=0, concat_axis=0, tiled=True)  49.1 us
    ppermute x1, waiting for transfers between devices, on_device(): after = lax.ppermute(edges, 'mem', [(i + 1, i) for i in range(ends)])  29.9 us
    all_to_all x2, waiting for transfers between devices, exchange(): lax.all_to_all(packed, 'mem', split_axis=0, concat_axis=0, tiled=True)  27.5 us
    all_to_all x2, starting transfers between devices, exchange(): lax.all_to_all(packed, 'mem', split_axis=0, concat_axis=0, tiled=True)  17.8 us
    unnamed x24, local copies, waits for them, and re-layouts  8.25 us
    pallas_call x1, Pallas kernels, on_device(): pl.pallas_call(first_kernel, out_shape=(shape(2, 3 * OWNED, MEMBERS, BLOC...  3.7 us
    ppermute x1, starting transfers between devices, on_device(): before = lax.ppermute(edges, 'mem', [(i, i + 1) for i in range(ends)])  3.2 us
  transfers between devices with their start and end apart: 4, of which 2 were waited for; matrix products, arithmetic and copies ran while one was open for 0% of the time, Pallas kernels for 3%

profile of v1, /device:TPU:1, one launch (start us, length us, event | category | flops | bytes accessed | tf_op | source)
XLA Modules:
  0.0 149.7 jit_solution(3982064676623163626)
XLA Ops:
  0.0 0.0 copy-start.3
  0.0 1.5 %slice_bitcast_fusion = (bf16[16,16384]{1,0:T(8,128)(2,1)S(1)}, bf16[16,16384]{1,0:T(8,128)(2,1)S(1)}, bf16[16,16384]{1,0:T(8,128)(2,1)S(1)}) fusion(bf16[3,16,16384]{2,1,0:T(8,128)(2,1)} %param.7), kind=kLoop, calls=%fused_computation | loop fusion | bytes 3145728 | tf_op jit(solution)/shard_map/squeeze | solution.py:129
  1.5 0.0 copy-done.3
  1.5 1.1 shard_map.73
  2.6 11.6 %all-to-all-start = ((bf16[64,2,16,256]{3,2,1,0:T(8,128)(2,1)}), bf16[64,2,16,256]{3,2,1,0:T(8,128)(2,1)S(1)}, u32[]{:S(2)}, u32[]{:S(2)}) async-start(bf16[64,2,16,256]{3,2,1,0:T(8,128)(2,1)} %shard_map.73), calls=%async_computation | async-start | bytes 2097152 | tf_op jit(solution)/shard_map/all_to_all | solution.py:124
  14.2 1.1 shard_map.76
  15.3 0.0 copy-start.8
  15.3 0.0 copy-start.9
  15.3 27.5 %all-to-all-done.arrived = bf16[64,2,16,256]{3,2,1,0:T(8,128)(2,1)S(1)} async-done(((bf16[64,2,16,256]{3,2,1,0:T(8,128)(2,1)}), bf16[64,2,16,256]{3,2,1,0:T(8,128)(2,1)S(1)}, u32[]{:S(2)}, u32[]{:S(2)}) %all-to-all-start) | async-done | bytes 1048608 | tf_op jit(solution)/shard_map/all_to_all | solution.py:124
  42.8 6.2 %all-to-all-start.1 = ((bf16[64,2,16,256]{3,2,1,0:T(8,128)(2,1)}), bf16[64,2,16,256]{3,2,1,0:T(8,128)(2,1)S(1)}, u32[]{:S(2)}, u32[]{:S(2)}) async-start(bf16[64,2,16,256]{3,2,1,0:T(8,128)(2,1)} %shard_map.76), calls=%async_computation.1 | async-start | bytes 2097152 | tf_op jit(solution)/shard_map/all_to_all | solution.py:124
  49.0 0.0 copy-start.11
  49.0 0.0 copy-start.10
  49.0 0.0 copy-done.8
  49.0 0.0 copy-done.9
  49.0 0.4 shard_map.74.middle
  49.5 2.4 %collective-permute-start.1 = (bf16[2,2,1024,128]{3,2,1,0:T(8,128)(2,1)S(1)}, bf16[2,2,1024,128]{3,2,1,0:T(8,128)(2,1)}, u32[]{:S(2)}, u32[]{:S(2)}) collective-permute-start(bf16[2,2,1024,128]{3,2,1,0:T(8,128)(2,1)S(1)} %shard_map.74.middle), channel_id=1, source_target_pairs={{8,0},{16,8},{24,16},{32,24},{40,32},{48,40},{56,48},{64,56},{72,6... | collective-permute-start | bytes 3145736 | tf_op jit(solution)/shard_map/ppermute | solution.py:139
  51.8 3.2 %collective-permute-start = (bf16[2,2,1024,128]{3,2,1,0:T(8,128)(2,1)S(1)}, bf16[2,2,1024,128]{3,2,1,0:T(8,128)(2,1)}, u32[]{:S(2)}, u32[]{:S(2)}) collective-permute-start(bf16[2,2,1024,128]{3,2,1,0:T(8,128)(2,1)S(1)} %shard_map.74.middle), channel_id=1, source_target_pairs={{0,8},{8,16},{16,24},{24,32},{32,40},{40,48},{48,56},{56,64},{64,7... | collective-permute-start | bytes 3145736 | tf_op jit(solution)/shard_map/ppermute | solution.py:138
  55.1 0.0 copy-done.11
  55.1 29.9 %collective-permute-done.1.after = bf16[2,2,1024,128]{3,2,1,0:T(8,128)(2,1)} collective-permute-done((bf16[2,2,1024,128]{3,2,1,0:T(8,128)(2,1)S(1)}, bf16[2,2,1024,128]{3,2,1,0:T(8,128)(2,1)}, u32[]{:S(2)}, u32[]{:S(2)}) %collective-permute-start.1) | collective-permute-done | bytes 1048608 | tf_op jit(solution)/shard_map/ppermute | solution.py:139
  85.0 0.0 collective-permute-done.before
  85.0 0.0 copy-done.10
  85.0 0.0 copy-start.2
  85.0 1.0 copy-done.2
  86.0 3.7 %shard_map.75 = (bf16[2,6,1024,128]{3,2,1,0:T(8,128)(2,1)S(1)}, f32[6,128,128]{2,1,0:T(8,128)S(1)}, f32[2,4,128,128]{3,2,1,0:T(8,128)S(1)}, bf16[64,16,256]{2,1,0:T(8,128)(2,1)S(1)}) custom-call(s32[2,4]{1,0:T(2,128)S(1)} %subtract_bitcast_fusion.index, s32[2,4]{1,0:T(2,128)S(1)} %bitcast.14, bf16[2,2,1024,128]{3,2,1,0:T(8,128)(2,1)} %collective-permute-done.before, ...), custom_call_target="tpu_custom_call" | custom-call | tf_op jit(solution)/shard_map/pallas_call | solution.py:141
  89.7 0.0 copy-start
  89.7 1.6 %copy-done = bf16[2,6,1024,128]{3,2,1,0:T(8,128)(2,1)} copy-done((bf16[2,6,1024,128]{3,2,1,0:T(8,128)(2,1)}, bf16[2,6,1024,128]{3,2,1,0:T(8,128)(2,1)S(1)}, u32[]{:S(2)}) %copy-start) | copy-done | bytes 3145752
  91.4 0.0 copy-start.4
  91.4 0.8 copy-done.4
  92.1 0.0 copy-start.6
  92.2 0.8 copy-done.6
  92.9 0.0 all-to-all-done.1.arrived
  92.9 0.0 copy-start.1
  92.9 1.9 %copy-done.1 = bf16[2,6,1024,128]{3,2,1,0:T(8,128)(2,1)S(1)} copy-done((bf16[2,6,1024,128]{3,2,1,0:T(8,128)(2,1)S(1)}, bf16[2,6,1024,128]{3,2,1,0:T(8,128)(2,1)}, u32[]{:S(2)}) %copy-start.1) | copy-done | bytes 3145752
  94.8 0.0 copy-start.5
  94.8 1.0 copy-done.5
  95.9 0.0 copy-start.7
  95.9 1.0 copy-done.7
  96.9 2.4 %shard_map.77 = bf16[64,3,16,256]{3,2,1,0:T(8,128)(2,1)S(1)} custom-call(s32[2,4]{1,0:T(2,128)S(1)} %subtract_bitcast_fusion.index, bf16[2,6,1024,128]{3,2,1,0:T(8,128)(2,1)S(1)} %copy-done.1, f32[6,128,128]{2,1,0:T(8,128)S(1)} %get-tuple-element.10.sums, f32[2,4,128,128]{3,2,1,0:T(8,128)S(1)} %copy-done.5, ...), custom_call_target="tpu_custom_call" | custom-call | tf_op jit(solution)/shard_map/pallas_call | solution.py:153
  99.4 49.1 %all_to_all.15 = bf16[64,3,16,256]{3,2,1,0:T(8,128)(2,1)S(1)} all-to-all(bf16[64,3,16,256]{3,2,1,0:T(8,128)(2,1)S(1)} %shard_map.77), channel_id=1, replica_groups=mesh['mem'=64,'patch'=8] {'mem'}, dimensions={0} | all-to-all | bytes 3145728 | tf_op jit(solution)/shard_map/all_to_all | solution.py:124
  148.5 1.2 copy.9
  (1 shorter events, 0.0 us)
Async XLA Ops:
  0.0 1.5 %copy-start.3 = (bf16[16,16384]{1,0:T(8,128)(2,1)S(1)}, bf16[16,16384]{1,0:T(8,128)(2,1)}, u32[]{:S(2)}) copy-start(bf16[16,16384]{1,0:T(8,128)(2,1)} %refs_1_.1) | copy-start | bytes 1572868
  2.6 40.2 %all-to-all-start = ((bf16[64,2,16,256]{3,2,1,0:T(8,128)(2,1)}), bf16[64,2,16,256]{3,2,1,0:T(8,128)(2,1)S(1)}, u32[]{:S(2)}, u32[]{:S(2)}) async-start(bf16[64,2,16,256]{3,2,1,0:T(8,128)(2,1)} %shard_map.73), calls=%async_computation | async-start | bytes 2097152 | tf_op jit(solution)/shard_map/all_to_all | solution.py:124
  15.3 33.7 %copy-start.8 = (bf16[1,2,128,128]{3,2,1,0:T(8,128)(2,1)S(1)}, bf16[1,2,128,128]{3,2,1,0:T(8,128)(2,1)}, u32[]{:S(2)}) copy-start(bf16[1,2,128,128]{3,2,1,0:T(8,128)(2,1)} %param.10) | copy-start | bytes 196612
  15.3 33.7 %copy-start.9 = (f32[1,256]{1,0:T(1,128)S(1)}, f32[1,256]{1,0:T(1,128)}, u32[]{:S(2)}) copy-start(f32[1,256]{1,0:T(1,128)} %obs.1) | copy-start | bytes 3076
  42.8 50.2 %all-to-all-start.1 = ((bf16[64,2,16,256]{3,2,1,0:T(8,128)(2,1)}), bf16[64,2,16,256]{3,2,1,0:T(8,128)(2,1)S(1)}, u32[]{:S(2)}, u32[]{:S(2)}) async-start(bf16[64,2,16,256]{3,2,1,0:T(8,128)(2,1)} %shard_map.76), calls=%async_computation.1 | async-start | bytes 2097152 | tf_op jit(solution)/shard_map/all_to_all | solution.py:124
  49.0 6.1 %copy-start.11 = (s32[1,2,4]{2,1,0:T(2,128)S(1)}, s32[1,2,4]{2,1,0:T(2,128)}, u32[]{:S(2)}) copy-start(s32[1,2,4]{2,1,0:T(2,128)} %param.12) | copy-start | bytes 100
  49.0 36.0 %copy-start.10 = (s32[1,2,4]{2,1,0:T(2,128)S(1)}, s32[1,2,4]{2,1,0:T(2,128)}, u32[]{:S(2)}) copy-start(s32[1,2,4]{2,1,0:T(2,128)} %param.13) | copy-start | bytes 100
  49.5 35.5 %collective-permute-start.1 = (bf16[2,2,1024,128]{3,2,1,0:T(8,128)(2,1)S(1)}, bf16[2,2,1024,128]{3,2,1,0:T(8,128)(2,1)}, u32[]{:S(2)}, u32[]{:S(2)}) collective-permute-start(bf16[2,2,1024,128]{3,2,1,0:T(8,128)(2,1)S(1)} %shard_map.74.middle), channel_id=1, source_target_pairs={{8,0},{16,8},{24,16},{32,24},{40,32},{48,40},{56,48},{64,56},{72,6... | collective-permute-start | bytes 3145736 | tf_op jit(solution)/shard_map/ppermute | solution.py:139
  51.8 33.1 %collective-permute-start = (bf16[2,2,1024,128]{3,2,1,0:T(8,128)(2,1)S(1)}, bf16[2,2,1024,128]{3,2,1,0:T(8,128)(2,1)}, u32[]{:S(2)}, u32[]{:S(2)}) collective-permute-start(bf16[2,2,1024,128]{3,2,1,0:T(8,128)(2,1)S(1)} %shard_map.74.middle), channel_id=1, source_target_pairs={{0,8},{8,16},{16,24},{24,32},{32,40},{40,48},{48,56},{56,64},{64,7... | collective-permute-start | bytes 3145736 | tf_op jit(solution)/shard_map/ppermute | solution.py:138
  85.0 1.0 copy-start.2
  89.7 1.6 %copy-start = (bf16[2,6,1024,128]{3,2,1,0:T(8,128)(2,1)}, bf16[2,6,1024,128]{3,2,1,0:T(8,128)(2,1)S(1)}, u32[]{:S(2)}) copy-start(bf16[2,6,1024,128]{3,2,1,0:T(8,128)(2,1)S(1)} %get-tuple-element.9.window) | copy-start | bytes 9437188
  91.4 0.8 copy-start.4
  92.1 0.8 copy-start.6
  92.9 1.9 %copy-start.1 = (bf16[2,6,1024,128]{3,2,1,0:T(8,128)(2,1)S(1)}, bf16[2,6,1024,128]{3,2,1,0:T(8,128)(2,1)}, u32[]{:S(2)}) copy-start(bf16[2,6,1024,128]{3,2,1,0:T(8,128)(2,1)} %copy-done) | copy-start | bytes 9437188
  94.8 1.0 copy-start.5
  95.9 1.0 copy-start.7

commit v2 on v1

v2 whole, which is shorter than its diff:
```python
import jax
import jax.numpy as jnp
from jax import lax
from jax.experimental import pallas as pl
from jax.experimental.pallas import tpu as pltpu
from jax.sharding import PartitionSpec as P

MEMBERS = 1024
VARIABLES = 3
BLOCK = 128
RADIUS = 2
PAIRS = 4
OWNED = 2
CELLS = OWNED * BLOCK
LOCAL_MEMBERS = 16
RING = 64
TILES = MEMBERS // BLOCK
PIECES = 4

VMEM = pl.BlockSpec(memory_space=pltpu.VMEM)
SMEM = pl.BlockSpec(memory_space=pltpu.SMEM)
HBM = pl.BlockSpec(memory_space=pltpu.HBM)
PARAMS = pltpu.CompilerParams(vmem_limit_bytes=40 * 1024 * 1024)
BF16 = jnp.bfloat16
F32 = jnp.float32


def shape(*dims, dtype=BF16):
    return jax.ShapeDtypeStruct(dims, dtype)


def prepare_kernel(arrived, obs, weights, edges):
    first = arrived[:, 0].reshape(MEMBERS, CELLS).astype(F32)
    noise = arrived[:, VARIABLES].reshape(MEMBERS, CELLS).astype(F32)
    mean = jnp.sum(first, axis=0, keepdims=True) * (1.0 / MEMBERS)
    anomaly = (first - mean).astype(BF16)
    innovation = (obs[...] + noise - first).astype(BF16)
    for block in range(OWNED):
        lanes = slice(block * BLOCK, (block + 1) * BLOCK)
        edges[1, block] = lax.dot_general(
            innovation[:, lanes],
            weights[block],
            (((1,), (1,)), ((), ())),
            preferred_element_type=F32,
        ).astype(BF16)
        for tile in range(TILES):
            rows = slice(tile * BLOCK, (tile + 1) * BLOCK)
            edges[0, block, rows] = anomaly[rows, lanes].T


def source_rows(window, source):
    tiles = [window[0, source, tile * BLOCK : (tile + 1) * BLOCK] for tile in range(TILES)]
    return jnp.concatenate(tiles, axis=1)


def center_kernel(arrived, centered):
    for variable in range(VARIABLES):
        wide = arrived[:, variable].reshape(MEMBERS, CELLS).astype(F32)
        mean = jnp.sum(wide, axis=0, keepdims=True) * (1.0 / MEMBERS)
        anomaly = (wide - mean).astype(BF16)
        for block in range(OWNED):
            lanes = slice(block * BLOCK, (block + 1) * BLOCK)
            centered[block, :, variable * BLOCK : (variable + 1) * BLOCK] = anomaly[:, lanes]


def taper_kernel(taper_at, table, tapers):
    for block in range(OWNED):
        for pair in range(PAIRS):
            tile = table[taper_at[block, pair]].T * (1.0 / (MEMBERS - 1))
            tapers[block, pair * BLOCK : (pair + 1) * BLOCK] = tile


def window_copies(parts, window, sems):
    copies = []
    for kind in range(2):
        for place, part in enumerate(parts):
            copies.append(
                pltpu.make_async_copy(
                    part.at[kind],
                    window.at[kind, pl.ds(place * OWNED, OWNED)],
                    sems.at[kind * 3 + place],
                )
            )
    return copies[:3], copies[3:]


def update_kernel(
    index, before, middle, after, arrived, centered, tapers, updated, window, out, sems
):
    anomalies, weighted = window_copies((before, middle, after), window, sems)
    for copy in anomalies + weighted:
        copy.start()
    sources = [[index[block, pair] for pair in range(PAIRS)] for block in range(OWNED)]
    for copy in anomalies:
        copy.wait()
    localized = []
    for block in range(OWNED):
        left = jnp.concatenate([source_rows(window, s) for s in sources[block]], axis=0)
        covariance = jnp.dot(left, centered[block], preferred_element_type=F32)
        taper = jnp.concatenate([tapers[block]] * VARIABLES, axis=1)
        localized.append((taper * covariance).astype(BF16))
    for copy in weighted:
        copy.wait()
    depth, owners = MEMBERS // PIECES, RING // PIECES
    leaving = []
    for piece in range(PIECES):
        rows = slice(piece * depth, (piece + 1) * depth)
        held = slice(piece * owners, (piece + 1) * owners)
        for block in range(OWNED):
            lanes = slice(block * BLOCK, (block + 1) * BLOCK)
            right = jnp.concatenate([window[1, s, rows] for s in sources[block]], axis=1)
            step = jnp.dot(right, localized[block], preferred_element_type=F32)
            for v in range(VARIABLES):
                base = arrived[held, v, :, lanes].reshape(depth, BLOCK).astype(F32)
                result = base + step[:, v * BLOCK : (v + 1) * BLOCK]
                out[held, v, :, lanes] = result.astype(BF16).reshape(owners, LOCAL_MEMBERS, BLOCK)
        part = pl.ds(piece * owners, owners)
        copy = pltpu.make_async_copy(out.at[part], updated.at[part], sems.at[6 + piece])
        copy.start()
        leaving.append(copy)
    for copy in leaving:
        copy.wait()


def pack_kernel(slots, *refs):
    count = len(slots)
    sources, out, held, sems = refs[: count], refs[count], refs[count + 1], refs[count + 2]
    width = RING * CELLS // PIECES
    copies = []
    for piece in range(PIECES):
        for slot, ref in enumerate(sources):
            lanes = pl.ds(piece * width, width)
            source = ref.at[:, lanes] if slots[slot] is None else ref.at[slots[slot], :, lanes]
            copies.append(
                pltpu.make_async_copy(
                    source, held.at[slot, :, lanes], sems.at[piece * count + slot]
                )
            )
    for copy in copies:
        copy.start()
    each = RING // PIECES
    for piece in range(PIECES):
        for slot in range(count):
            copies[piece * count + slot].wait()
            for rank in range(piece * each, (piece + 1) * each):
                lanes = slice(rank * CELLS, (rank + 1) * CELLS)
                out[rank, slot] = held[slot, :, lanes]


def pack(*arrays):
    count = len(arrays)

    def kernel(*refs):
        pack_kernel([slot for _, slot in arrays], *refs)

    return pl.pallas_call(
        kernel,
        out_shape=pltpu.HBM((RING, count, LOCAL_MEMBERS, CELLS), BF16),
        in_specs=[HBM] * count,
        out_specs=VMEM,
        scratch_shapes=[
            pltpu.VMEM((count, LOCAL_MEMBERS, RING * CELLS), BF16),
            pltpu.SemaphoreType.DMA((PIECES * count,)),
        ],
        compiler_params=PARAMS,
    )(*[in_hbm(array) for array, _ in arrays])


def unpack_kernel(back, out, held, sems):
    width, each = RING * CELLS // PIECES, RING // PIECES
    copies = []
    for piece in range(PIECES):
        for rank in range(piece * each, (piece + 1) * each):
            held[:, :, rank * CELLS : (rank + 1) * CELLS] = back[rank]
        lanes = pl.ds(piece * width, width)
        copy = pltpu.make_async_copy(held.at[:, :, lanes], out.at[:, :, lanes], sems.at[piece])
        copy.start()
        copies.append(copy)
    for copy in copies:
        copy.wait()


def unpack(back):
    return pl.pallas_call(
        unpack_kernel,
        out_shape=pltpu.HBM((VARIABLES, LOCAL_MEMBERS, RING * CELLS), BF16),
        in_specs=[VMEM],
        out_specs=HBM,
        scratch_shapes=[
            pltpu.VMEM((VARIABLES, LOCAL_MEMBERS, RING * CELLS), BF16),
            pltpu.SemaphoreType.DMA((PIECES,)),
        ],
        compiler_params=PARAMS,
    )(back)


def in_hbm(array):
    return pltpu.with_memory_space_constraint(array, pltpu.HBM)


def exchange(packed):
    return lax.all_to_all(packed, "mem", split_axis=0, concat_axis=0, tiled=True)


def on_device(state, obs_noise, obs_values, obs_weights, tapers, pair_source, pair_taper):
    arrived = exchange(pack((state, 0), (state, 1), (state, 2), (obs_noise, None)))
    edges = pl.pallas_call(
        prepare_kernel,
        out_shape=shape(2, OWNED, MEMBERS, BLOCK),
        in_specs=[VMEM] * 3,
        out_specs=VMEM,
        compiler_params=PARAMS,
    )(arrived, obs_values, obs_weights[0])
    ends = RING - 1
    before = lax.ppermute(edges, "mem", [(i, i + 1) for i in range(ends)])
    after = lax.ppermute(edges, "mem", [(i + 1, i) for i in range(ends)])
    centered = pl.pallas_call(
        center_kernel,
        out_shape=shape(OWNED, MEMBERS, VARIABLES * BLOCK),
        in_specs=[VMEM],
        out_specs=VMEM,
        compiler_params=PARAMS,
    )(arrived)
    taper_tiles = pl.pallas_call(
        taper_kernel,
        out_shape=shape(OWNED, PAIRS * BLOCK, BLOCK, dtype=F32),
        in_specs=[SMEM, VMEM],
        out_specs=VMEM,
        compiler_params=PARAMS,
    )(pair_taper[0], tapers)
    index = pair_source[0] - (lax.axis_index("mem") * OWNED - RADIUS)
    updated = pl.pallas_call(
        update_kernel,
        out_shape=pltpu.HBM((RING, VARIABLES, LOCAL_MEMBERS, CELLS), BF16),
        in_specs=[SMEM] + [HBM] * 3 + [VMEM] * 3,
        out_specs=HBM,
        scratch_shapes=[
            pltpu.VMEM((2, 3 * OWNED, MEMBERS, BLOCK), BF16),
            pltpu.VMEM((RING, VARIABLES, LOCAL_MEMBERS, CELLS), BF16),
            pltpu.SemaphoreType.DMA((6 + PIECES,)),
        ],
        compiler_params=PARAMS,
    )(index, in_hbm(before), in_hbm(edges), in_hbm(after), arrived, centered, taper_tiles)
    return unpack(exchange(updated))


def solution(mesh):
    placed = (
        P(None, "mem", "patch"),
        P("mem", "patch"),
        P("patch", "mem"),
        P("patch", "mem", None, None),
        P(),
        P("patch", "mem", None),
        P("patch", "mem", None),
    )
    return jax.shard_map(
        on_device, mesh=mesh, in_specs=placed, out_specs=P(None, "mem", "patch"), check_vma=False
    )
```

time: 150 us -> 140 us (0.933)
  blocking collectives: 49.1 us -> 112 us
  waiting for transfers between devices: 57.4 us -> 9.22 us
  starting transfers between devices: 23.4 us -> 5.56 us
  local copies, waits for them, and re-layouts: 11 us -> 1.06 us
  Pallas kernels: 8.71 us -> 11.4 us
    all_to_all x1 -> x2, blocking collectives: 49.1 us -> 112 us  [exchange(): lax.all_to_all(packed, 'mem', split_axis=0, concat_axis=0, tiled=True)]
    all_to_all x2 -> x0, waiting for transfers between devices: 27.5 us -> none  [exchange(): lax.all_to_all(packed, 'mem', split_axis=0, concat_axis=0, tiled=True)]
    ppermute x1, waiting for transfers between devices: 29.9 us -> 8.14 us  [on_device(): after = lax.ppermute(edges, 'mem', [(i + 1, i) for i in range(ends)])]
    all_to_all x2 -> x0, starting transfers between devices: 17.8 us -> none  [exchange(): lax.all_to_all(packed, 'mem', split_axis=0, concat_axis=0, tiled=True)]
    unnamed x24 -> x12, local copies, waits for them, and re-layouts: 8.25 us -> 1.06 us
    pallas_call x4 -> x5, Pallas kernels: 8.27 us -> 10.9 us  [the longest x1 5.26 us: on_device(): pl.pallas_call(update_kernel, out_shape=pltpu.HBM((RING, VARIABLES, LOCAL...]
    squeeze x1 -> x0, local copies, waits for them, and re-layouts: 1.52 us -> none  [on_device(): others = exchange(pack(state[1], state[2]))]
  transfers between devices with their start and end apart: 4 -> 2, of which waited for: 2 -> 2; matrix products, arithmetic and copies ran while one was open for 0% -> 0% of each run, Pallas kernels for 3% -> 1%
where the time goes in v2:
time: 140 us; the launch traced here: 139 us
  blocking collectives  112 us (80%)
  Pallas kernels  11.4 us (8%)
  waiting for transfers between devices  9.22 us (7%)
  starting transfers between devices  5.56 us (4%)
    all_to_all x2, blocking collectives, exchange(): lax.all_to_all(packed, 'mem', split_axis=0, concat_axis=0, tiled=True)  112 us
    ppermute x1, waiting for transfers between devices, on_device(): after = lax.ppermute(edges, 'mem', [(i + 1, i) for i in range(ends)])  8.14 us
    pallas_call x1, Pallas kernels, on_device(): pl.pallas_call(update_kernel, out_shape=pltpu.HBM((RING, VARIABLES, LOCAL...  5.26 us
    ppermute x1, starting transfers between devices, on_device(): before = lax.ppermute(edges, 'mem', [(i, i + 1) for i in range(ends)])  3.26 us
    pallas_call x1, Pallas kernels, pack(): pl.pallas_call(kernel, out_shape=pltpu.HBM((RING, count, LOCAL_MEMBERS, C...  3.09 us
  transfers between devices with their start and end apart: 2, of which 2 were waited for; matrix products, arithmetic and copies ran while one was open for 0% of the time, Pallas kernels for 1%

profile of v2, /device:TPU:1, one launch (start us, length us, event | category | flops | bytes accessed | tf_op | source)
XLA Modules:
  0.0 139.3 jit_solution(15583557220912387195)
XLA Ops:
  0.0 3.1 %shard_map.73 = bf16[64,4,16,256]{3,2,1,0:T(8,128)(2,1)} custom-call(bf16[3,16,16384]{2,1,0:T(8,128)(2,1)} %refs_2_.1, bf16[3,16,16384]{2,1,0:T(8,128)(2,1)} %refs_2_.1, bf16[3,16,16384]{2,1,0:T(8,128)(2,1)} %refs_2_.1, bf16[16,16384]{1,0:T(8,128)(2,1)} %refs_3_.1), custom_call_target="tpu_custom_call" | custom-call | tf_op jit(solution)/shard_map/pallas_call | solution.py:156
  3.1 0.0 copy-start.2
  3.1 0.0 copy-start.3
  3.1 63.0 %all_to_all.10.arrived = bf16[64,4,16,256]{3,2,1,0:T(8,128)(2,1)S(1)} all-to-all(bf16[64,4,16,256]{3,2,1,0:T(8,128)(2,1)} %shard_map.73), channel_id=1, replica_groups=mesh['mem'=64,'patch'=8] {'mem'}, dimensions={0} | all-to-all | bytes 4194304 | tf_op jit(solution)/shard_map/all_to_all | solution.py:202
  66.1 0.0 copy-done.2
  66.1 0.0 copy-done.3
  66.1 0.0 copy-start.4
  66.1 0.0 copy-start.5
  66.1 0.4 shard_map.74.middle
  66.6 0.0 copy-start
  66.6 2.3 %collective-permute-start.1 = (bf16[2,2,1024,128]{3,2,1,0:T(8,128)(2,1)S(1)}, bf16[2,2,1024,128]{3,2,1,0:T(8,128)(2,1)}, u32[]{:S(2)}, u32[]{:S(2)}) collective-permute-start(bf16[2,2,1024,128]{3,2,1,0:T(8,128)(2,1)S(1)} %shard_map.74.middle), channel_id=1, source_target_pairs={{8,0},{16,8},{24,16},{32,24},{40,32},{48,40},{56,48},{64,56},{72,6... | collective-permute-start | bytes 3145736 | tf_op jit(solution)/shard_map/ppermute | solution.py:216
  68.9 3.3 %collective-permute-start = (bf16[2,2,1024,128]{3,2,1,0:T(8,128)(2,1)S(1)}, bf16[2,2,1024,128]{3,2,1,0:T(8,128)(2,1)}, u32[]{:S(2)}, u32[]{:S(2)}) collective-permute-start(bf16[2,2,1024,128]{3,2,1,0:T(8,128)(2,1)S(1)} %shard_map.74.middle), channel_id=1, source_target_pairs={{0,8},{8,16},{16,24},{24,32},{32,40},{40,48},{48,56},{56,64},{64,7... | collective-permute-start | bytes 3145736 | tf_op jit(solution)/shard_map/ppermute | solution.py:215
  72.2 0.0 copy-done.4
  72.2 0.0 copy-start.1
  72.2 1.0 copy-done.1
  73.2 0.8 shard_map.76.tapers
  74.0 0.0 copy-done.5
  74.0 0.6 shard_map.75.centered
  74.7 0.0 copy-done
  74.7 8.1 %collective-permute-done.1.after = bf16[2,2,1024,128]{3,2,1,0:T(8,128)(2,1)} collective-permute-done((bf16[2,2,1024,128]{3,2,1,0:T(8,128)(2,1)S(1)}, bf16[2,2,1024,128]{3,2,1,0:T(8,128)(2,1)}, u32[]{:S(2)}, u32[]{:S(2)}) %collective-permute-start.1) | collective-permute-done | bytes 1048608 | tf_op jit(solution)/shard_map/ppermute | solution.py:216
  82.8 1.1 collective-permute-done.before
  83.9 5.3 %shard_map.77 = bf16[64,3,16,256]{3,2,1,0:T(8,128)(2,1)} custom-call(s32[2,4]{1,0:T(2,128)S(1)} %subtract_bitcast_fusion.index, bf16[2,2,1024,128]{3,2,1,0:T(8,128)(2,1)} %collective-permute-done.before, bf16[2,2,1024,128]{3,2,1,0:T(8,128)(2,1)} %copy-done, bf16[2,2,1024,128]{3,2,1,0:T(8,128)(2,1)} %collective-permute-done.1.after, ...), custom_call_target="tpu_custom_call" | custom-call | tf_op jit(solution)/shard_map/pallas_call | solution.py:232
  89.2 48.9 %all_to_all.11.back = bf16[64,3,16,256]{3,2,1,0:T(8,128)(2,1)S(1)} all-to-all(bf16[64,3,16,256]{3,2,1,0:T(8,128)(2,1)} %shard_map.77), channel_id=1, replica_groups=mesh['mem'=64,'patch'=8] {'mem'}, dimensions={0} | all-to-all | bytes 3145728 | tf_op jit(solution)/shard_map/all_to_all | solution.py:202
  138.1 1.2 shard_map.78
  (1 shorter events, 0.0 us)
Async XLA Ops:
  3.1 63.0 %copy-start.2 = (bf16[1,2,128,128]{3,2,1,0:T(8,128)(2,1)S(1)}, bf16[1,2,128,128]{3,2,1,0:T(8,128)(2,1)}, u32[]{:S(2)}) copy-start(bf16[1,2,128,128]{3,2,1,0:T(8,128)(2,1)} %param.10) | copy-start | bytes 196612
  3.1 63.0 %copy-start.3 = (f32[1,256]{1,0:T(1,128)S(1)}, f32[1,256]{1,0:T(1,128)}, u32[]{:S(2)}) copy-start(f32[1,256]{1,0:T(1,128)} %obs.1) | copy-start | bytes 3076
  66.1 6.1 %copy-start.4 = (s32[1,2,4]{2,1,0:T(2,128)S(1)}, s32[1,2,4]{2,1,0:T(2,128)}, u32[]{:S(2)}) copy-start(s32[1,2,4]{2,1,0:T(2,128)} %param.13) | copy-start | bytes 100
  66.1 7.9 %copy-start.5 = (s32[1,2,4]{2,1,0:T(2,128)S(1)}, s32[1,2,4]{2,1,0:T(2,128)}, u32[]{:S(2)}) copy-start(s32[1,2,4]{2,1,0:T(2,128)} %param.12) | copy-start | bytes 100
  66.6 8.1 %copy-start = (bf16[2,2,1024,128]{3,2,1,0:T(8,128)(2,1)}, bf16[2,2,1024,128]{3,2,1,0:T(8,128)(2,1)S(1)}, u32[]{:S(2)}) copy-start(bf16[2,2,1024,128]{3,2,1,0:T(8,128)(2,1)S(1)} %shard_map.74.middle) | copy-start | bytes 3145732
  66.6 16.2 %collective-permute-start.1 = (bf16[2,2,1024,128]{3,2,1,0:T(8,128)(2,1)S(1)}, bf16[2,2,1024,128]{3,2,1,0:T(8,128)(2,1)}, u32[]{:S(2)}, u32[]{:S(2)}) collective-permute-start(bf16[2,2,1024,128]{3,2,1,0:T(8,128)(2,1)S(1)} %shard_map.74.middle), channel_id=1, source_target_pairs={{8,0},{16,8},{24,16},{32,24},{40,32},{48,40},{56,48},{64,56},{72,6... | collective-permute-start | bytes 3145736 | tf_op jit(solution)/shard_map/ppermute | solution.py:216
  68.9 15.0 %collective-permute-start = (bf16[2,2,1024,128]{3,2,1,0:T(8,128)(2,1)S(1)}, bf16[2,2,1024,128]{3,2,1,0:T(8,128)(2,1)}, u32[]{:S(2)}, u32[]{:S(2)}) collective-permute-start(bf16[2,2,1024,128]{3,2,1,0:T(8,128)(2,1)S(1)} %shard_map.74.middle), channel_id=1, source_target_pairs={{0,8},{8,16},{16,24},{24,32},{32,40},{40,48},{48,56},{56,64},{64,7... | collective-permute-start | bytes 3145736 | tf_op jit(solution)/shard_map/ppermute | solution.py:215
  72.2 1.0 copy-start.1

commit v3 on v2

v3 whole, which is shorter than its diff:
```python
import jax
import jax.numpy as jnp
from jax import lax
from jax.experimental import pallas as pl
from jax.experimental.pallas import tpu as pltpu
from jax.sharding import PartitionSpec as P

MEMBERS = 1024
VARIABLES = 3
BLOCK = 128
RADIUS = 2
PAIRS = 4
OWNED = 2
CELLS = OWNED * BLOCK
LOCAL_MEMBERS = 16
RING = 64
TILES = MEMBERS // BLOCK
PIECES = 4

VMEM = pl.BlockSpec(memory_space=pltpu.VMEM)
SMEM = pl.BlockSpec(memory_space=pltpu.SMEM)
HBM = pl.BlockSpec(memory_space=pltpu.HBM)
PARAMS = pltpu.CompilerParams(vmem_limit_bytes=40 * 1024 * 1024)
BF16 = jnp.bfloat16
F32 = jnp.float32


def shape(*dims, dtype=BF16):
    return jax.ShapeDtypeStruct(dims, dtype)


def prepare_kernel(arrived, obs, weights, tapers, anomalies, weighted):
    del tapers
    first = arrived[:, 0].reshape(MEMBERS, CELLS).astype(F32)
    noise = arrived[:, VARIABLES].reshape(MEMBERS, CELLS).astype(F32)
    mean = jnp.sum(first, axis=0, keepdims=True) * (1.0 / MEMBERS)
    anomaly = (first - mean).astype(BF16)
    innovation = (obs[...] + noise - first).astype(BF16)
    for block in range(OWNED):
        lanes = slice(block * BLOCK, (block + 1) * BLOCK)
        for tile in range(TILES):
            rows = slice(tile * BLOCK, (tile + 1) * BLOCK)
            anomalies[block, rows] = anomaly[rows, lanes].T
        weighted[block] = lax.dot_general(
            innovation[:, lanes],
            weights[block],
            (((1,), (1,)), ((), ())),
            preferred_element_type=F32,
        ).astype(BF16)


def source_rows(window, source):
    tiles = [window[source, tile * BLOCK : (tile + 1) * BLOCK] for tile in range(TILES)]
    return jnp.concatenate(tiles, axis=1)


def center_kernel(arrived, centered):
    for variable in range(VARIABLES):
        wide = arrived[:, variable].reshape(MEMBERS, CELLS).astype(F32)
        mean = jnp.sum(wide, axis=0, keepdims=True) * (1.0 / MEMBERS)
        anomaly = (wide - mean).astype(BF16)
        for block in range(OWNED):
            lanes = slice(block * BLOCK, (block + 1) * BLOCK)
            centered[block, :, variable * BLOCK : (variable + 1) * BLOCK] = anomaly[:, lanes]


def taper_kernel(taper_at, table, tapers):
    for block in range(OWNED):
        for pair in range(PAIRS):
            tile = table[taper_at[block, pair]].T * (1.0 / (MEMBERS - 1))
            tapers[block, pair * BLOCK : (pair + 1) * BLOCK] = tile


def localize_kernel(index, across, own, mate, centered, tapers, localized, window):
    window[:OWNED] = across[...]
    window[OWNED : 2 * OWNED] = own[...]
    window[2 * OWNED :] = mate[...]
    for block in range(OWNED):
        sources = [index[block, pair] for pair in range(PAIRS)]
        left = jnp.concatenate([source_rows(window, s) for s in sources], axis=0)
        covariance = jnp.dot(left, centered[block], preferred_element_type=F32)
        taper = jnp.concatenate([tapers[block]] * VARIABLES, axis=1)
        localized[block] = (taper * covariance).astype(BF16)


def update_kernel(index, across, own, mate, arrived, localized, updated, window, out, out_sems):
    depth, owners = MEMBERS // PIECES, RING // PIECES
    sources = [[index[block, pair] for pair in range(PAIRS)] for block in range(OWNED)]
    leaving = []
    for piece in range(PIECES):
        rows = slice(piece * depth, (piece + 1) * depth)
        held = slice(piece * owners, (piece + 1) * owners)
        window[:OWNED, rows] = across[:, rows]
        window[OWNED : 2 * OWNED, rows] = own[:, rows]
        window[2 * OWNED :, rows] = mate[:, rows]
        for block in range(OWNED):
            lanes = slice(block * BLOCK, (block + 1) * BLOCK)
            right = jnp.concatenate([window[s, rows] for s in sources[block]], axis=1)
            step = jnp.dot(right, localized[block], preferred_element_type=F32)
            for v in range(VARIABLES):
                base = arrived[held, v, :, lanes].reshape(depth, BLOCK).astype(F32)
                result = base + step[:, v * BLOCK : (v + 1) * BLOCK]
                out[held, v, :, lanes] = result.astype(BF16).reshape(owners, LOCAL_MEMBERS, BLOCK)
        part = pl.ds(piece * owners, owners)
        copy = pltpu.make_async_copy(out.at[part], updated.at[part], out_sems.at[piece])
        copy.start()
        leaving.append(copy)
    for copy in leaving:
        copy.wait()


def pack_kernel(state, noise, packed, held, out, sems, out_sems):
    width, each = RING * CELLS // PIECES, RING // PIECES
    entering = []
    for piece in range(PIECES):
        lanes = pl.ds(piece * width, width)
        pair = (
            pltpu.make_async_copy(
                state.at[:, :, lanes], held.at[pl.ds(0, VARIABLES), :, lanes], sems.at[2 * piece]
            ),
            pltpu.make_async_copy(
                noise.at[:, lanes], held.at[VARIABLES, :, lanes], sems.at[2 * piece + 1]
            ),
        )
        for copy in pair:
            copy.start()
        entering.append(pair)
    leaving = []
    for piece in range(PIECES):
        for copy in entering[piece]:
            copy.wait()
        for rank in range(piece * each, (piece + 1) * each):
            out[rank] = held[:, :, rank * CELLS : (rank + 1) * CELLS]
        part = pl.ds(piece * each, each)
        copy = pltpu.make_async_copy(out.at[part], packed.at[part], out_sems.at[piece])
        copy.start()
        leaving.append(copy)
    for copy in leaving:
        copy.wait()


def pack(state, noise):
    count = VARIABLES + 1
    return pl.pallas_call(
        pack_kernel,
        out_shape=pltpu.HBM((RING, count, LOCAL_MEMBERS, CELLS), BF16),
        in_specs=[HBM] * 2,
        out_specs=HBM,
        scratch_shapes=[
            pltpu.VMEM((count, LOCAL_MEMBERS, RING * CELLS), BF16),
            pltpu.VMEM((RING, count, LOCAL_MEMBERS, CELLS), BF16),
            pltpu.SemaphoreType.DMA((2 * PIECES,)),
            pltpu.SemaphoreType.DMA((PIECES,)),
        ],
        compiler_params=PARAMS,
    )(in_hbm(state), in_hbm(noise))


def unpack_kernel(back, out, held, sems):
    width, each = RING * CELLS // PIECES, RING // PIECES
    copies = []
    for piece in range(PIECES):
        for rank in range(piece * each, (piece + 1) * each):
            held[:, :, rank * CELLS : (rank + 1) * CELLS] = back[rank]
        lanes = pl.ds(piece * width, width)
        copy = pltpu.make_async_copy(held.at[:, :, lanes], out.at[:, :, lanes], sems.at[piece])
        copy.start()
        copies.append(copy)
    for copy in copies:
        copy.wait()


def unpack(back):
    return pl.pallas_call(
        unpack_kernel,
        out_shape=pltpu.HBM((VARIABLES, LOCAL_MEMBERS, RING * CELLS), BF16),
        in_specs=[VMEM],
        out_specs=HBM,
        scratch_shapes=[
            pltpu.VMEM((VARIABLES, LOCAL_MEMBERS, RING * CELLS), BF16),
            pltpu.SemaphoreType.DMA((PIECES,)),
        ],
        compiler_params=PARAMS,
    )(back)


def in_hbm(array):
    return pltpu.with_memory_space_constraint(array, pltpu.HBM)


def exchange(packed):
    return lax.all_to_all(packed, "mem", split_axis=0, concat_axis=0, tiled=True)


def on_device(state, obs_noise, obs_values, obs_weights, tapers, pair_source, pair_taper):
    arrived = exchange(pack(state, obs_noise))
    half = (OWNED, MEMBERS, BLOCK)
    taper_tiles = pl.pallas_call(
        taper_kernel,
        out_shape=shape(OWNED, PAIRS * BLOCK, BLOCK, dtype=F32),
        in_specs=[SMEM, VMEM],
        out_specs=VMEM,
        compiler_params=PARAMS,
    )(pair_taper[0], tapers)
    anomalies, weighted = pl.pallas_call(
        prepare_kernel,
        out_shape=(shape(*half), shape(*half)),
        in_specs=[VMEM] * 4,
        out_specs=(VMEM,) * 2,
        compiler_params=PARAMS,
    )(arrived, obs_values, obs_weights[0], taper_tiles)
    across = [(i, i + 1) for i in range(1, RING - 1, 2)]
    across += [(j, i) for i, j in across]
    inside = [(i, i ^ 1) for i in range(RING)]
    across_anomalies = lax.ppermute(anomalies, "mem", across)
    across_weighted = lax.ppermute(weighted, "mem", across)
    centered = pl.pallas_call(
        center_kernel,
        out_shape=shape(OWNED, MEMBERS, VARIABLES * BLOCK),
        in_specs=[VMEM],
        out_specs=VMEM,
        compiler_params=PARAMS,
    )(arrived)
    mate_anomalies = lax.ppermute(anomalies, "mem", inside)
    mate_weighted = lax.ppermute(weighted, "mem", inside)
    place = lax.axis_index("mem")
    index = pair_source[0] - (place * OWNED - RADIUS)
    turn = jnp.where(place % 2 == 1, 2 * OWNED, 0)
    index = jnp.where(index < OWNED, index + turn, jnp.where(index < 2 * OWNED, index, index - turn))
    window = pltpu.VMEM((3 * OWNED, MEMBERS, BLOCK), BF16)
    localized = pl.pallas_call(
        localize_kernel,
        out_shape=shape(OWNED, PAIRS * BLOCK, VARIABLES * BLOCK),
        in_specs=[SMEM] + [VMEM] * 5,
        out_specs=VMEM,
        scratch_shapes=[window],
        compiler_params=PARAMS,
    )(index, across_anomalies, anomalies, mate_anomalies, centered, taper_tiles)
    updated = pl.pallas_call(
        update_kernel,
        out_shape=pltpu.HBM((RING, VARIABLES, LOCAL_MEMBERS, CELLS), BF16),
        in_specs=[SMEM] + [VMEM] * 5,
        out_specs=HBM,
        scratch_shapes=[
            window,
            pltpu.VMEM((RING, VARIABLES, LOCAL_MEMBERS, CELLS), BF16),
            pltpu.SemaphoreType.DMA((PIECES,)),
        ],
        compiler_params=PARAMS,
    )(index, across_weighted, weighted, mate_weighted, arrived, localized)
    return unpack(exchange(updated))


def solution(mesh):
    placed = (
        P(None, "mem", "patch"),
        P("mem", "patch"),
        P("patch", "mem"),
        P("patch", "mem", None, None),
        P(),
        P("patch", "mem", None),
        P("patch", "mem", None),
    )
    return jax.shard_map(
        on_device, mesh=mesh, in_specs=placed, out_specs=P(None, "mem", "patch"), check_vma=False
    )
```

time: 140 us -> 135 us (0.964)
  blocking collectives: 112 us -> 46.8 us
  waiting for transfers between devices: 9.22 us -> 53.9 us
  starting transfers between devices: 5.56 us -> 21.3 us
    all_to_all x2 -> x1, blocking collectives: 112 us -> 46.8 us  [exchange(): lax.all_to_all(packed, 'mem', split_axis=0, concat_axis=0, tiled=True)]
    all_to_all x0 -> x1, waiting for transfers between devices: none -> 50.5 us  [exchange(): lax.all_to_all(packed, 'mem', split_axis=0, concat_axis=0, tiled=True)]
    all_to_all x0 -> x1, starting transfers between devices: none -> 11.8 us  [exchange(): lax.all_to_all(packed, 'mem', split_axis=0, concat_axis=0, tiled=True)]
    ppermute x2 -> x4, waiting for transfers between devices: 9.22 us -> 3.43 us  [the longest x1 2.9 us: on_device(): across_weighted = lax.ppermute(weighted, 'mem', across)]
    ppermute x2 -> x4, starting transfers between devices: 5.56 us -> 9.57 us  [the longest x1 3.64 us: on_device(): across_weighted = lax.ppermute(weighted, 'mem', across)]
    pallas_call x2 -> x3, Pallas kernels: 3.53 us -> 6.46 us  [the longest x1 2.71 us: on_device(): pl.pallas_call(localize_kernel, out_shape=shape(OWNED, PAIRS * BLOCK, VAR...]
    pallas_call x1, Pallas kernels: 5.26 us -> 3.38 us  [on_device(): pl.pallas_call(update_kernel, out_shape=pltpu.HBM((RING, VARIABLES, LOCAL...]
  transfers between devices with their start and end apart: 2 -> 5, of which waited for: 2 -> 3; matrix products, arithmetic and copies ran while one was open for 0% -> 0% of each run, Pallas kernels for 1% -> 3%
where the time goes in v3:
time: 135 us
  waiting for transfers between devices  53.9 us (40%)
  blocking collectives  46.8 us (35%)
  starting transfers between devices  21.3 us (16%)
  Pallas kernels  12.4 us (9%)
    all_to_all x1, waiting for transfers between devices, exchange(): lax.all_to_all(packed, 'mem', split_axis=0, concat_axis=0, tiled=True)  50.5 us
    all_to_all x1, blocking collectives, exchange(): lax.all_to_all(packed, 'mem', split_axis=0, concat_axis=0, tiled=True)  46.8 us
    all_to_all x1, starting transfers between devices, exchange(): lax.all_to_all(packed, 'mem', split_axis=0, concat_axis=0, tiled=True)  11.8 us
    ppermute x1, starting transfers between devices, on_device(): across_weighted = lax.ppermute(weighted, 'mem', across)  3.64 us
    pallas_call x1, Pallas kernels, on_device(): pl.pallas_call(update_kernel, out_shape=pltpu.HBM((RING, VARIABLES, LOCAL...  3.38 us
    ppermute x1, waiting for transfers between devices, on_device(): across_weighted = lax.ppermute(weighted, 'mem', across)  2.9 us
    pallas_call x1, Pallas kernels, on_device(): pl.pallas_call(localize_kernel, out_shape=shape(OWNED, PAIRS * BLOCK, VAR...  2.71 us
  transfers between devices with their start and end apart: 5, of which 3 were waited for; matrix products, arithmetic and copies ran while one was open for 0% of the time, Pallas kernels for 3%

profile of v3, /device:TPU:1, one launch (start us, length us, event | category | flops | bytes accessed | tf_op | source)
XLA Modules:
  0.0 134.7 jit_solution(3207020842754489382)
XLA Ops:
  0.0 2.5 %shard_map.73 = bf16[64,4,16,256]{3,2,1,0:T(8,128)(2,1)} custom-call(bf16[3,16,16384]{2,1,0:T(8,128)(2,1)} %state.1, bf16[16,16384]{1,0:T(8,128)(2,1)} %noise.1), custom_call_target="tpu_custom_call" | custom-call | tf_op jit(solution)/shard_map/pallas_call | solution.py:144
  2.5 0.0 copy-start
  2.5 0.0 copy-start.3
  2.5 0.0 copy-start.1
  2.6 0.0 copy-start.2
  2.6 11.8 %all-to-all-start = ((bf16[64,4,16,256]{3,2,1,0:T(8,128)(2,1)}), bf16[64,4,16,256]{3,2,1,0:T(8,128)(2,1)S(1)}, u32[]{:S(2)}, u32[]{:S(2)}) async-start(bf16[64,4,16,256]{3,2,1,0:T(8,128)(2,1)} %shard_map.73), calls=%async_computation | async-start | bytes 4194304 | tf_op jit(solution)/shard_map/all_to_all | solution.py:192
  14.3 0.0 copy-done
  14.4 0.0 copy-done.3
  14.4 0.8 shard_map.74.tapers
  15.1 0.0 copy-start.4
  15.1 50.5 %all-to-all-done.arrived = bf16[64,4,16,256]{3,2,1,0:T(8,128)(2,1)S(1)} async-done(((bf16[64,4,16,256]{3,2,1,0:T(8,128)(2,1)}), bf16[64,4,16,256]{3,2,1,0:T(8,128)(2,1)S(1)}, u32[]{:S(2)}, u32[]{:S(2)}) %all-to-all-start) | async-done | bytes 2097184 | tf_op jit(solution)/shard_map/all_to_all | solution.py:192
  65.6 0.0 copy-done.1
  65.6 0.0 copy-done.2
  65.6 1.2 shard_map.75
  66.8 2.1 %collective-permute-start.2 = (bf16[2,1024,128]{2,1,0:T(8,128)(2,1)}, bf16[2,1024,128]{2,1,0:T(8,128)(2,1)}, u32[]{:S(2)}, u32[]{:S(2)}) collective-permute-start(bf16[2,1024,128]{2,1,0:T(8,128)(2,1)} %get-tuple-element.8.own), channel_id=1, source_target_pairs={{8,16},{24,32},{40,48},{56,64},{72,80},{88,96},{104,112},{120,128}... | collective-permute-start | bytes 1572872 | tf_op jit(solution)/shard_map/ppermute | solution.py:215
  68.9 1.9 %collective-permute-start.3 = (bf16[2,1024,128]{2,1,0:T(8,128)(2,1)}, bf16[2,1024,128]{2,1,0:T(8,128)(2,1)}, u32[]{:S(2)}, u32[]{:S(2)}) collective-permute-start(bf16[2,1024,128]{2,1,0:T(8,128)(2,1)} %get-tuple-element.8.own), channel_id=1, source_target_pairs={{0,8},{8,0},{16,24},{24,16},{32,40},{40,32},{48,56},{56,48},{64,72... | collective-permute-start | bytes 1572872 | tf_op jit(solution)/shard_map/ppermute | solution.py:224
  70.8 3.6 %collective-permute-start = (bf16[2,1024,128]{2,1,0:T(8,128)(2,1)S(1)}, bf16[2,1024,128]{2,1,0:T(8,128)(2,1)}, u32[]{:S(2)}, u32[]{:S(2)}) collective-permute-start(bf16[2,1024,128]{2,1,0:T(8,128)(2,1)S(1)} %get-tuple-element.7.own), channel_id=1, source_target_pairs={{8,16},{24,32},{40,48},{56,64},{72,80},{88,96},{104,112},{120,128}... | collective-permute-start | bytes 1572872 | tf_op jit(solution)/shard_map/ppermute | solution.py:216
  74.5 1.9 %collective-permute-start.1 = (bf16[2,1024,128]{2,1,0:T(8,128)(2,1)S(1)}, bf16[2,1024,128]{2,1,0:T(8,128)(2,1)}, u32[]{:S(2)}, u32[]{:S(2)}) collective-permute-start(bf16[2,1024,128]{2,1,0:T(8,128)(2,1)S(1)} %get-tuple-element.7.own), channel_id=1, source_target_pairs={{0,8},{8,0},{16,24},{24,16},{32,40},{40,32},{48,56},{56,48},{64,72... | collective-permute-start | bytes 1572872 | tf_op jit(solution)/shard_map/ppermute | solution.py:225
  76.4 0.0 copy-done.4
  76.5 0.6 shard_map.76.centered
  77.1 0.5 collective-permute-done.2.across
  77.6 0.0 collective-permute-done.3.mate
  77.6 2.7 %shard_map.77.localized = bf16[2,512,384]{2,1,0:T(8,128)(2,1)S(1)} custom-call(s32[2,4]{1,0:T(2,128)S(1)} %compare_select_fusion.1.index, bf16[2,1024,128]{2,1,0:T(8,128)(2,1)} %collective-permute-done.2.across, bf16[2,1024,128]{2,1,0:T(8,128)(2,1)} %get-tuple-element.8.own, bf16[2,1024,128]{2,1,0:T(8,128)(2,1)} %collective-permute-done.3.mate, ...), custom_call_target="tpu_custom_call" | custom-call | tf_op jit(solution)/shard_map/pallas_call | solution.py:231
  80.4 2.9 %collective-permute-done.across = bf16[2,1024,128]{2,1,0:T(8,128)(2,1)} collective-permute-done((bf16[2,1024,128]{2,1,0:T(8,128)(2,1)S(1)}, bf16[2,1024,128]{2,1,0:T(8,128)(2,1)}, u32[]{:S(2)}, u32[]{:S(2)}) %collective-permute-start) | collective-permute-done | bytes 524320 | tf_op jit(solution)/shard_map/ppermute | solution.py:216
  83.3 0.0 collective-permute-done.1.mate
  83.3 3.4 %shard_map.78 = bf16[64,3,16,256]{3,2,1,0:T(8,128)(2,1)} custom-call(s32[2,4]{1,0:T(2,128)S(1)} %compare_select_fusion.1.index, bf16[2,1024,128]{2,1,0:T(8,128)(2,1)} %collective-permute-done.across, bf16[2,1024,128]{2,1,0:T(8,128)(2,1)S(1)} %get-tuple-element.7.own, bf16[2,1024,128]{2,1,0:T(8,128)(2,1)} %collective-permute-done.1.mate, ...), custom_call_target="tpu_custom_call" | custom-call | tf_op jit(solution)/shard_map/pallas_call | solution.py:239
  86.6 46.8 %all_to_all.10.back = bf16[64,3,16,256]{3,2,1,0:T(8,128)(2,1)S(1)} all-to-all(bf16[64,3,16,256]{3,2,1,0:T(8,128)(2,1)} %shard_map.78), channel_id=1, replica_groups=mesh['mem'=64,'patch'=8] {'mem'}, dimensions={0} | all-to-all | bytes 3145728 | tf_op jit(solution)/shard_map/all_to_all | solution.py:192
  133.5 1.2 shard_map.79
  (1 shorter events, 0.0 us)
Async XLA Ops:
  2.5 11.8 %copy-start = (f32[8,128,128]{2,1,0:T(8,128)S(1)}, f32[8,128,128]{2,1,0:T(8,128)}, u32[]{:S(2)}) copy-start(f32[8,128,128]{2,1,0:T(8,128)} %table.1) | copy-start | bytes 1572868
  2.5 11.8 %copy-start.3 = (s32[1,2,4]{2,1,0:T(2,128)S(1)}, s32[1,2,4]{2,1,0:T(2,128)}, u32[]{:S(2)}) copy-start(s32[1,2,4]{2,1,0:T(2,128)} %param.13) | copy-start | bytes 100
  2.5 63.0 %copy-start.1 = (bf16[1,2,128,128]{3,2,1,0:T(8,128)(2,1)S(1)}, bf16[1,2,128,128]{3,2,1,0:T(8,128)(2,1)}, u32[]{:S(2)}) copy-start(bf16[1,2,128,128]{3,2,1,0:T(8,128)(2,1)} %param.10) | copy-start | bytes 196612
  2.6 63.0 %copy-start.2 = (f32[1,256]{1,0:T(1,128)S(1)}, f32[1,256]{1,0:T(1,128)}, u32[]{:S(2)}) copy-start(f32[1,256]{1,0:T(1,128)} %obs.1) | copy-start | bytes 3076
  2.6 63.0 %all-to-all-start = ((bf16[64,4,16,256]{3,2,1,0:T(8,128)(2,1)}), bf16[64,4,16,256]{3,2,1,0:T(8,128)(2,1)S(1)}, u32[]{:S(2)}, u32[]{:S(2)}) async-start(bf16[64,4,16,256]{3,2,1,0:T(8,128)(2,1)} %shard_map.73), calls=%async_computation | async-start | bytes 4194304 | tf_op jit(solution)/shard_map/all_to_all | solution.py:192
  15.1 61.3 %copy-start.4 = (s32[1,2,4]{2,1,0:T(2,128)S(1)}, s32[1,2,4]{2,1,0:T(2,128)}, u32[]{:S(2)}) copy-start(s32[1,2,4]{2,1,0:T(2,128)} %param.12) | copy-start | bytes 100
  66.8 10.8 %collective-permute-start.2 = (bf16[2,1024,128]{2,1,0:T(8,128)(2,1)}, bf16[2,1024,128]{2,1,0:T(8,128)(2,1)}, u32[]{:S(2)}, u32[]{:S(2)}) collective-permute-start(bf16[2,1024,128]{2,1,0:T(8,128)(2,1)} %get-tuple-element.8.own), channel_id=1, source_target_pairs={{8,16},{24,32},{40,48},{56,64},{72,80},{88,96},{104,112},{120,128}... | collective-permute-start | bytes 1572872 | tf_op jit(solution)/shard_map/ppermute | solution.py:215
  68.9 8.7 %collective-permute-start.3 = (bf16[2,1024,128]{2,1,0:T(8,128)(2,1)}, bf16[2,1024,128]{2,1,0:T(8,128)(2,1)}, u32[]{:S(2)}, u32[]{:S(2)}) collective-permute-start(bf16[2,1024,128]{2,1,0:T(8,128)(2,1)} %get-tuple-element.8.own), channel_id=1, source_target_pairs={{0,8},{8,0},{16,24},{24,16},{32,40},{40,32},{48,56},{56,48},{64,72... | collective-permute-start | bytes 1572872 | tf_op jit(solution)/shard_map/ppermute | solution.py:224
  70.8 12.4 %collective-permute-start = (bf16[2,1024,128]{2,1,0:T(8,128)(2,1)S(1)}, bf16[2,1024,128]{2,1,0:T(8,128)(2,1)}, u32[]{:S(2)}, u32[]{:S(2)}) collective-permute-start(bf16[2,1024,128]{2,1,0:T(8,128)(2,1)S(1)} %get-tuple-element.7.own), channel_id=1, source_target_pairs={{8,16},{24,32},{40,48},{56,64},{72,80},{88,96},{104,112},{120,128}... | collective-permute-start | bytes 1572872 | tf_op jit(solution)/shard_map/ppermute | solution.py:216
  74.5 8.8 %collective-permute-start.1 = (bf16[2,1024,128]{2,1,0:T(8,128)(2,1)S(1)}, bf16[2,1024,128]{2,1,0:T(8,128)(2,1)}, u32[]{:S(2)}, u32[]{:S(2)}) collective-permute-start(bf16[2,1024,128]{2,1,0:T(8,128)(2,1)S(1)} %get-tuple-element.7.own), channel_id=1, source_target_pairs={{0,8},{8,0},{16,24},{24,16},{32,40},{40,32},{48,56},{56,48},{64,72... | collective-permute-start | bytes 1572872 | tf_op jit(solution)/shard_map/ppermute | solution.py:225

commit v4 on v3

--- a/solution.py
+++ b/solution.py
@@ -29,7 +29,7 @@
     return jax.ShapeDtypeStruct(dims, dtype)
 
 
-def prepare_kernel(arrived, obs, weights, tapers, anomalies, weighted):
+def prepare_kernel(arrived, obs, weights, tapers, edges, anomalies, weighted):
     del tapers
     first = arrived[:, 0].reshape(MEMBERS, CELLS).astype(F32)
     noise = arrived[:, VARIABLES].reshape(MEMBERS, CELLS).astype(F32)
@@ -40,18 +40,23 @@
         lanes = slice(block * BLOCK, (block + 1) * BLOCK)
         for tile in range(TILES):
             rows = slice(tile * BLOCK, (tile + 1) * BLOCK)
-            anomalies[block, rows] = anomaly[rows, lanes].T
-        weighted[block] = lax.dot_general(
+            turned = anomaly[rows, lanes].T
+            edges[0, block, rows] = turned
+            anomalies[block, rows] = turned
+        product = lax.dot_general(
             innovation[:, lanes],
             weights[block],
             (((1,), (1,)), ((), ())),
             preferred_element_type=F32,
         ).astype(BF16)
-
-
-def source_rows(window, source):
-    tiles = [window[source, tile * BLOCK : (tile + 1) * BLOCK] for tile in range(TILES)]
-    return jnp.concatenate(tiles, axis=1)
+        edges[1, block] = product
+        weighted[block] = product
+
+
+def member_columns(part, block):
+    return jnp.concatenate(
+        [part[block, tile * BLOCK : (tile + 1) * BLOCK] for tile in range(TILES)], axis=1
+    )
 
 
 def center_kernel(arrived, centered):
@@ -64,43 +69,64 @@
             centered[block, :, variable * BLOCK : (variable + 1) * BLOCK] = anomaly[:, lanes]
 
 
-def taper_kernel(taper_at, table, tapers):
+def taper_kernel(index, taper_at, table, tapers):
     for block in range(OWNED):
-        for pair in range(PAIRS):
-            tile = table[taper_at[block, pair]].T * (1.0 / (MEMBERS - 1))
-            tapers[block, pair * BLOCK : (pair + 1) * BLOCK] = tile
-
-
-def localize_kernel(index, across, own, mate, centered, tapers, localized, window):
-    window[:OWNED] = across[...]
-    window[OWNED : 2 * OWNED] = own[...]
-    window[2 * OWNED :] = mate[...]
-    for block in range(OWNED):
-        sources = [index[block, pair] for pair in range(PAIRS)]
-        left = jnp.concatenate([source_rows(window, s) for s in sources], axis=0)
-        covariance = jnp.dot(left, centered[block], preferred_element_type=F32)
-        taper = jnp.concatenate([tapers[block]] * VARIABLES, axis=1)
-        localized[block] = (taper * covariance).astype(BF16)
-
-
-def update_kernel(index, across, own, mate, arrived, localized, updated, window, out, out_sems):
+        tiles = [table[taper_at[block, pair]].T * (1.0 / (MEMBERS - 1)) for pair in range(PAIRS)]
+        for source in range(3 * OWNED):
+            total = jnp.zeros((BLOCK, BLOCK), F32)
+            for pair in range(PAIRS):
+                total += tiles[pair] * jnp.where(index[block, pair] == source, 1.0, 0.0)
+            tapers[block, source * BLOCK : (source + 1) * BLOCK] = total
+
+
+def localized_part(left, centered, tapers):
+    covariance = jnp.dot(left, centered, preferred_element_type=F32)
+    return (jnp.concatenate([tapers] * VARIABLES, axis=1) * covariance).astype(BF16)
+
+
+def near_kernel(own, mate, own_weighted, mate_weighted, centered, tapers, arrived, partial):
     depth, owners = MEMBERS // PIECES, RING // PIECES
-    sources = [[index[block, pair] for pair in range(PAIRS)] for block in range(OWNED)]
-    leaving = []
+    left = jnp.concatenate(
+        [member_columns(part, block) for part in (own, mate) for block in range(OWNED)], axis=0
+    )
+    localized = [
+        localized_part(left, centered[block], tapers[block, OWNED * BLOCK :])
+        for block in range(OWNED)
+    ]
     for piece in range(PIECES):
         rows = slice(piece * depth, (piece + 1) * depth)
         held = slice(piece * owners, (piece + 1) * owners)
-        window[:OWNED, rows] = across[:, rows]
-        window[OWNED : 2 * OWNED, rows] = own[:, rows]
-        window[2 * OWNED :, rows] = mate[:, rows]
+        right = jnp.concatenate(
+            [part[b, rows] for part in (own_weighted, mate_weighted) for b in range(OWNED)], axis=1
+        )
         for block in range(OWNED):
             lanes = slice(block * BLOCK, (block + 1) * BLOCK)
-            right = jnp.concatenate([window[s, rows] for s in sources[block]], axis=1)
             step = jnp.dot(right, localized[block], preferred_element_type=F32)
             for v in range(VARIABLES):
                 base = arrived[held, v, :, lanes].reshape(depth, BLOCK).astype(F32)
-                result = base + step[:, v * BLOCK : (v + 1) * BLOCK]
-                out[held, v, :, lanes] = result.astype(BF16).reshape(owners, LOCAL_MEMBERS, BLOCK)
+                columns = slice(v * BLOCK, (v + 1) * BLOCK)
+                partial[block, rows, columns] = base + step[:, columns]
+
+
+def far_kernel(across, centered, tapers, partial, updated, out, out_sems):
+    depth, owners = MEMBERS // PIECES, RING // PIECES
+    leaving = []
+    left = jnp.concatenate([member_columns(across.at[0], b) for b in range(OWNED)], axis=0)
+    localized = [
+        localized_part(left, centered[block], tapers[block, : OWNED * BLOCK])
+        for block in range(OWNED)
+    ]
+    for piece in range(PIECES):
+        rows = slice(piece * depth, (piece + 1) * depth)
+        held = slice(piece * owners, (piece + 1) * owners)
+        right = jnp.concatenate([across[1, block, rows] for block in range(OWNED)], axis=1)
+        for block in range(OWNED):
+            lanes = slice(block * BLOCK, (block + 1) * BLOCK)
+            step = jnp.dot(right, localized[block], preferred_element_type=F32)
+            result = (partial[block, rows] + step).astype(BF16)
+            for v in range(VARIABLES):
+                columns = slice(v * BLOCK, (v + 1) * BLOCK)
+                out[held, v, :, lanes] = result[:, columns].reshape(owners, LOCAL_MEMBERS, BLOCK)
         part = pl.ds(piece * owners, owners)
         copy = pltpu.make_async_copy(out.at[part], updated.at[part], out_sems.at[piece])
         copy.start()
@@ -195,25 +221,30 @@
 def on_device(state, obs_noise, obs_values, obs_weights, tapers, pair_source, pair_taper):
     arrived = exchange(pack(state, obs_noise))
     half = (OWNED, MEMBERS, BLOCK)
-    taper_tiles = pl.pallas_call(
+    place = lax.axis_index("mem")
+    index = pair_source[0] - (place * OWNED - RADIUS)
+    turn = jnp.where(place % 2 == 1, 2 * OWNED, 0)
+    index = jnp.where(index < OWNED, index + turn, jnp.where(index < 2 * OWNED, index, index - turn))
+    taper_sums = pl.pallas_call(
         taper_kernel,
-        out_shape=shape(OWNED, PAIRS * BLOCK, BLOCK, dtype=F32),
-        in_specs=[SMEM, VMEM],
+        out_shape=shape(OWNED, 3 * OWNED * BLOCK, BLOCK, dtype=F32),
+        in_specs=[SMEM, SMEM, VMEM],
         out_specs=VMEM,
         compiler_params=PARAMS,
-    )(pair_taper[0], tapers)
-    anomalies, weighted = pl.pallas_call(
+    )(index, pair_taper[0], tapers)
+    edges, anomalies, weighted = pl.pallas_call(
         prepare_kernel,
-        out_shape=(shape(*half), shape(*half)),
+        out_shape=(shape(2, *half), shape(*half), shape(*half)),
         in_specs=[VMEM] * 4,
-        out_specs=(VMEM,) * 2,
-        compiler_params=PARAMS,
-    )(arrived, obs_values, obs_weights[0], taper_tiles)
+        out_specs=(VMEM,) * 3,
+        compiler_params=PARAMS,
+    )(arrived, obs_values, obs_weights[0], taper_sums)
     across = [(i, i + 1) for i in range(1, RING - 1, 2)]
     across += [(j, i) for i, j in across]
     inside = [(i, i ^ 1) for i in range(RING)]
-    across_anomalies = lax.ppermute(anomalies, "mem", across)
-    across_weighted = lax.ppermute(weighted, "mem", across)
+    far = lax.ppermute(edges, "mem", across)
+    mate_anomalies = lax.ppermute(anomalies, "mem", inside)
+    mate_weighted = lax.ppermute(weighted, "mem", inside)
     centered = pl.pallas_call(
         center_kernel,
         out_shape=shape(OWNED, MEMBERS, VARIABLES * BLOCK),
@@ -221,33 +252,24 @@
         out_specs=VMEM,
         compiler_params=PARAMS,
     )(arrived)
-    mate_anomalies = lax.ppermute(anomalies, "mem", inside)
-    mate_weighted = lax.ppermute(weighted, "mem", inside)
-    place = lax.axis_index("mem")
-    index = pair_source[0] - (place * OWNED - RADIUS)
-    turn = jnp.where(place % 2 == 1, 2 * OWNED, 0)
-    index = jnp.where(index < OWNED, index + turn, jnp.where(index < 2 * OWNED, index, index - turn))
-    window = pltpu.VMEM((3 * OWNED, MEMBERS, BLOCK), BF16)
-    localized = pl.pallas_call(
-        localize_kernel,
-        out_shape=shape(OWNED, PAIRS * BLOCK, VARIABLES * BLOCK),
-        in_specs=[SMEM] + [VMEM] * 5,
+    partial = pl.pallas_call(
+        near_kernel,
+        out_shape=shape(OWNED, MEMBERS, VARIABLES * BLOCK, dtype=F32),
+        in_specs=[VMEM] * 7,
         out_specs=VMEM,
-        scratch_shapes=[window],
-        compiler_params=PARAMS,
-    )(index, across_anomalies, anomalies, mate_anomalies, centered, taper_tiles)
+        compiler_params=PARAMS,
+    )(anomalies, mate_anomalies, weighted, mate_weighted, centered, taper_sums, arrived)
     updated = pl.pallas_call(
-        update_kernel,
+        far_kernel,
         out_shape=pltpu.HBM((RING, VARIABLES, LOCAL_MEMBERS, CELLS), BF16),
-        in_specs=[SMEM] + [VMEM] * 5,
+        in_specs=[VMEM] * 4,
         out_specs=HBM,
         scratch_shapes=[
-            window,
             pltpu.VMEM((RING, VARIABLES, LOCAL_MEMBERS, CELLS), BF16),
             pltpu.SemaphoreType.DMA((PIECES,)),
         ],
         compiler_params=PARAMS,
-    )(index, across_weighted, weighted, mate_weighted, arrived, localized)
+    )(far, centered, taper_sums, partial)
     return unpack(exchange(updated))
 
 

time: 135 us -> 133 us (0.985)
  starting transfers between devices: 21.3 us -> 18.2 us
  waiting for transfers between devices: 53.9 us -> 57 us
  Pallas kernels: 12.4 us -> 10.1 us
    ppermute x2 -> x1, starting transfers between devices: 5.72 us -> 2.09 us  [on_device(): far = lax.ppermute(edges, 'mem', across)]
    ppermute x2 -> x1, waiting for transfers between devices: 3.42 us -> 5.8 us  [on_device(): far = lax.ppermute(edges, 'mem', across)]
    pallas_call x4, Pallas kernels: 8.08 us -> 5.77 us  [the longest x1 2.35 us: on_device(): pl.pallas_call(near_kernel, out_shape=shape(OWNED, MEMBERS, VARIABLES * B...]
  transfers between devices with their start and end apart: 5 -> 4, of which waited for: 3 -> 3; matrix products, arithmetic and copies ran while one was open for 0% -> 0% of each run, Pallas kernels for 3% -> 3%
where the time goes in v4:
time: 133 us; the launch traced here: 132 us
  waiting for transfers between devices  57 us (43%)
  blocking collectives  46.8 us (35%)
  starting transfers between devices  18.2 us (14%)
  Pallas kernels  10.1 us (8%)
    all_to_all x1, waiting for transfers between devices, exchange(): lax.all_to_all(packed, 'mem', split_axis=0, concat_axis=0, tiled=True)  50.3 us
    all_to_all x1, blocking collectives, exchange(): lax.all_to_all(packed, 'mem', split_axis=0, concat_axis=0, tiled=True)  46.8 us
    all_to_all x1, starting transfers between devices, exchange(): lax.all_to_all(packed, 'mem', split_axis=0, concat_axis=0, tiled=True)  11.8 us
    ppermute x1, waiting for transfers between devices, on_device(): far = lax.ppermute(edges, 'mem', across)  5.8 us
  transfers between devices with their start and end apart: 4, of which 3 were waited for; matrix products, arithmetic and copies ran while one was open for 0% of the time, Pallas kernels for 3%

profile of v4, /device:TPU:1, one launch (start us, length us, event | category | flops | bytes accessed | tf_op | source)
XLA Modules:
  0.0 132.3 jit_solution(13348901368013497318)
XLA Ops:
  0.0 2.5 %shard_map.73 = bf16[64,4,16,256]{3,2,1,0:T(8,128)(2,1)} custom-call(bf16[3,16,16384]{2,1,0:T(8,128)(2,1)} %state.1, bf16[16,16384]{1,0:T(8,128)(2,1)} %noise.1), custom_call_target="tpu_custom_call" | custom-call | tf_op jit(solution)/shard_map/pallas_call | solution.py:170
  2.5 0.0 copy-start.4
  2.5 0.0 copy-start
  2.6 0.0 copy-start.2
  2.6 0.0 copy-start.1
  2.6 0.0 copy-start.3
  2.6 11.8 %all-to-all-start = ((bf16[64,4,16,256]{3,2,1,0:T(8,128)(2,1)}), bf16[64,4,16,256]{3,2,1,0:T(8,128)(2,1)S(1)}, u32[]{:S(2)}, u32[]{:S(2)}) async-start(bf16[64,4,16,256]{3,2,1,0:T(8,128)(2,1)} %shard_map.73), calls=%async_computation | async-start | bytes 4194304 | tf_op jit(solution)/shard_map/all_to_all | solution.py:218
  14.4 0.0 copy-done.4
  14.4 0.0 copy-done
  14.4 0.0 copy-done.2
  14.4 0.8 shard_map.74.tapers
  15.3 50.3 %all-to-all-done.arrived = bf16[64,4,16,256]{3,2,1,0:T(8,128)(2,1)S(1)} async-done(((bf16[64,4,16,256]{3,2,1,0:T(8,128)(2,1)}), bf16[64,4,16,256]{3,2,1,0:T(8,128)(2,1)S(1)}, u32[]{:S(2)}, u32[]{:S(2)}) %all-to-all-start) | async-done | bytes 2097184 | tf_op jit(solution)/shard_map/all_to_all | solution.py:218
  65.6 0.0 copy-done.1
  65.6 0.0 copy-done.3
  65.6 0.5 shard_map.75
  66.1 2.1 %collective-permute-start = (bf16[2,2,1024,128]{3,2,1,0:T(8,128)(2,1)S(1)}, bf16[2,2,1024,128]{3,2,1,0:T(8,128)(2,1)S(1)}, u32[]{:S(2)}, u32[]{:S(2)}) collective-permute-start(bf16[2,2,1024,128]{3,2,1,0:T(8,128)(2,1)S(1)} %get-tuple-element.8), channel_id=1, source_target_pairs={{8,16},{24,32},{40,48},{56,64},{72,80},{88,96},{104,112},{120,128}... | collective-permute-start | bytes 3145736 | tf_op jit(solution)/shard_map/ppermute | solution.py:245
  68.2 1.9 %collective-permute-start.1 = (bf16[2,1024,128]{2,1,0:T(8,128)(2,1)S(1)}, bf16[2,1024,128]{2,1,0:T(8,128)(2,1)S(1)}, u32[]{:S(2)}, u32[]{:S(2)}) collective-permute-start(bf16[2,1024,128]{2,1,0:T(8,128)(2,1)S(1)} %get-tuple-element.9.own), channel_id=1, source_target_pairs={{0,8},{8,0},{16,24},{24,16},{32,40},{40,32},{48,56},{56,48},{64,72... | collective-permute-start | bytes 1572872 | tf_op jit(solution)/shard_map/ppermute | solution.py:246
  70.1 2.4 %collective-permute-start.2 = (bf16[2,1024,128]{2,1,0:T(8,128)(2,1)S(1)}, bf16[2,1024,128]{2,1,0:T(8,128)(2,1)S(1)}, u32[]{:S(2)}, u32[]{:S(2)}) collective-permute-start(bf16[2,1024,128]{2,1,0:T(8,128)(2,1)S(1)} %get-tuple-element.10.own_weighted), channel_id=1, source_target_pairs={{0,8},{8,0},{16,24},{24,16},{32,40},{40,32},{48,56},{56,48},{64,72... | collective-permute-start | bytes 1572872 | tf_op jit(solution)/shard_map/ppermute | solution.py:247
  72.5 0.6 shard_map.76.centered
  73.2 0.0 collective-permute-done.1.mate
  73.2 0.9 collective-permute-done.2.mate_weighted
  74.1 2.4 %shard_map.77.partial = f32[2,1024,384]{2,1,0:T(8,128)S(1)} custom-call(bf16[2,1024,128]{2,1,0:T(8,128)(2,1)S(1)} %get-tuple-element.9.own, bf16[2,1024,128]{2,1,0:T(8,128)(2,1)S(1)} %collective-permute-done.1.mate, bf16[2,1024,128]{2,1,0:T(8,128)(2,1)S(1)} %get-tuple-element.10.own_weighted, bf16[2,1024,128]{2,1,0:T(8,128)(2,1)S(1)} %collective-permute-done.2.mate_weighted, ...), custom_call_target="tpu_custom_call" | custom-call | tf_op jit(solution)/shard_map/pallas_call | solution.py:255
  76.4 5.8 %collective-permute-done.across = bf16[2,2,1024,128]{3,2,1,0:T(8,128)(2,1)S(1)} collective-permute-done((bf16[2,2,1024,128]{3,2,1,0:T(8,128)(2,1)S(1)}, bf16[2,2,1024,128]{3,2,1,0:T(8,128)(2,1)S(1)}, u32[]{:S(2)}, u32[]{:S(2)}) %collective-permute-start) | collective-permute-done | bytes 1048608 | tf_op jit(solution)/shard_map/ppermute | solution.py:245
  82.2 2.1 %shard_map.78 = bf16[64,3,16,256]{3,2,1,0:T(8,128)(2,1)} custom-call(bf16[2,2,1024,128]{3,2,1,0:T(8,128)(2,1)S(1)} %collective-permute-done.across, bf16[2,1024,384]{2,1,0:T(8,128)(2,1)S(1)} %shard_map.76.centered, f32[2,768,128]{2,1,0:T(8,128)S(1)} %shard_map.74.tapers, f32[2,1024,384]{2,1,0:T(8,128)S(1)} %shard_map.77.partial), custom_call_target="tpu_custom_call" | custom-call | tf_op jit(solution)/shard_map/pallas_call | solution.py:262
  84.3 46.8 %all_to_all.10.back = bf16[64,3,16,256]{3,2,1,0:T(8,128)(2,1)S(1)} all-to-all(bf16[64,3,16,256]{3,2,1,0:T(8,128)(2,1)} %shard_map.78), channel_id=1, replica_groups=mesh['mem'=64,'patch'=8] {'mem'}, dimensions={0} | all-to-all | bytes 3145728 | tf_op jit(solution)/shard_map/all_to_all | solution.py:218
  131.2 1.2 shard_map.79
  (1 shorter events, 0.0 us)
Async XLA Ops:
  2.5 11.8 %copy-start.4 = (s32[1,2,4]{2,1,0:T(2,128)S(1)}, s32[1,2,4]{2,1,0:T(2,128)}, u32[]{:S(2)}) copy-start(s32[1,2,4]{2,1,0:T(2,128)} %param.12) | copy-start | bytes 100
  2.5 11.9 %copy-start = (f32[8,128,128]{2,1,0:T(8,128)S(1)}, f32[8,128,128]{2,1,0:T(8,128)}, u32[]{:S(2)}) copy-start(f32[8,128,128]{2,1,0:T(8,128)} %table.1) | copy-start | bytes 1572868
  2.6 11.9 %copy-start.2 = (s32[1,2,4]{2,1,0:T(2,128)S(1)}, s32[1,2,4]{2,1,0:T(2,128)}, u32[]{:S(2)}) copy-start(s32[1,2,4]{2,1,0:T(2,128)} %param.13) | copy-start | bytes 100
  2.6 63.0 %copy-start.1 = (bf16[1,2,128,128]{3,2,1,0:T(8,128)(2,1)S(1)}, bf16[1,2,128,128]{3,2,1,0:T(8,128)(2,1)}, u32[]{:S(2)}) copy-start(bf16[1,2,128,128]{3,2,1,0:T(8,128)(2,1)} %param.10) | copy-start | bytes 196612
  2.6 63.0 %copy-start.3 = (f32[1,256]{1,0:T(1,128)S(1)}, f32[1,256]{1,0:T(1,128)}, u32[]{:S(2)}) copy-start(f32[1,256]{1,0:T(1,128)} %obs.1) | copy-start | bytes 3076
  2.6 63.0 %all-to-all-start = ((bf16[64,4,16,256]{3,2,1,0:T(8,128)(2,1)}), bf16[64,4,16,256]{3,2,1,0:T(8,128)(2,1)S(1)}, u32[]{:S(2)}, u32[]{:S(2)}) async-start(bf16[64,4,16,256]{3,2,1,0:T(8,128)(2,1)} %shard_map.73), calls=%async_computation | async-start | bytes 4194304 | tf_op jit(solution)/shard_map/all_to_all | solution.py:218
  66.1 16.1 %collective-permute-start = (bf16[2,2,1024,128]{3,2,1,0:T(8,128)(2,1)S(1)}, bf16[2,2,1024,128]{3,2,1,0:T(8,128)(2,1)S(1)}, u32[]{:S(2)}, u32[]{:S(2)}) collective-permute-start(bf16[2,2,1024,128]{3,2,1,0:T(8,128)(2,1)S(1)} %get-tuple-element.8), channel_id=1, source_target_pairs={{8,16},{24,32},{40,48},{56,64},{72,80},{88,96},{104,112},{120,128}... | collective-permute-start | bytes 3145736 | tf_op jit(solution)/shard_map/ppermute | solution.py:245
  68.2 5.0 %collective-permute-start.1 = (bf16[2,1024,128]{2,1,0:T(8,128)(2,1)S(1)}, bf16[2,1024,128]{2,1,0:T(8,128)(2,1)S(1)}, u32[]{:S(2)}, u32[]{:S(2)}) collective-permute-start(bf16[2,1024,128]{2,1,0:T(8,128)(2,1)S(1)} %get-tuple-element.9.own), channel_id=1, source_target_pairs={{0,8},{8,0},{16,24},{24,16},{32,40},{40,32},{48,56},{56,48},{64,72... | collective-permute-start | bytes 1572872 | tf_op jit(solution)/shard_map/ppermute | solution.py:246
  70.1 3.9 %collective-permute-start.2 = (bf16[2,1024,128]{2,1,0:T(8,128)(2,1)S(1)}, bf16[2,1024,128]{2,1,0:T(8,128)(2,1)S(1)}, u32[]{:S(2)}, u32[]{:S(2)}) collective-permute-start(bf16[2,1024,128]{2,1,0:T(8,128)(2,1)S(1)} %get-tuple-element.10.own_weighted), channel_id=1, source_target_pairs={{0,8},{8,0},{16,24},{24,16},{32,40},{40,32},{48,56},{56,48},{64,72... | collective-permute-start | bytes 1572872 | tf_op jit(solution)/shard_map/ppermute | solution.py:247

commit v5 on v4

--- a/solution.py
+++ b/solution.py
@@ -108,21 +108,21 @@
                 partial[block, rows, columns] = base + step[:, columns]
 
 
-def far_kernel(across, centered, tapers, partial, updated, out, out_sems):
+def far_kernel(core, across, centered, tapers, partial, updated, out, out_sems):
     depth, owners = MEMBERS // PIECES, RING // PIECES
+    both, one = core[0], 1 - core[0]
+    first = jnp.concatenate([member_columns(across.at[0], b) for b in range(OWNED)], axis=0)
+    wide = localized_part(first, centered[both], tapers[both, : OWNED * BLOCK])
+    near_rows = pl.ds(pl.multiple_of(one * BLOCK, BLOCK), BLOCK)
+    narrow = localized_part(member_columns(across.at[0], one), centered[one], tapers[one, near_rows])
     leaving = []
-    left = jnp.concatenate([member_columns(across.at[0], b) for b in range(OWNED)], axis=0)
-    localized = [
-        localized_part(left, centered[block], tapers[block, : OWNED * BLOCK])
-        for block in range(OWNED)
-    ]
     for piece in range(PIECES):
         rows = slice(piece * depth, (piece + 1) * depth)
         held = slice(piece * owners, (piece + 1) * owners)
         right = jnp.concatenate([across[1, block, rows] for block in range(OWNED)], axis=1)
-        for block in range(OWNED):
-            lanes = slice(block * BLOCK, (block + 1) * BLOCK)
-            step = jnp.dot(right, localized[block], preferred_element_type=F32)
+        for block, weighted, localized in ((both, right, wide), (one, across[1, one, rows], narrow)):
+            lanes = pl.ds(pl.multiple_of(block * BLOCK, BLOCK), BLOCK)
+            step = jnp.dot(weighted, localized, preferred_element_type=F32)
             result = (partial[block, rows] + step).astype(BF16)
             for v in range(VARIABLES):
                 columns = slice(v * BLOCK, (v + 1) * BLOCK)
@@ -262,14 +262,14 @@
     updated = pl.pallas_call(
         far_kernel,
         out_shape=pltpu.HBM((RING, VARIABLES, LOCAL_MEMBERS, CELLS), BF16),
-        in_specs=[VMEM] * 4,
+        in_specs=[SMEM] + [VMEM] * 4,
         out_specs=HBM,
         scratch_shapes=[
             pltpu.VMEM((RING, VARIABLES, LOCAL_MEMBERS, CELLS), BF16),
             pltpu.SemaphoreType.DMA((PIECES,)),
         ],
         compiler_params=PARAMS,
-    )(far, centered, taper_sums, partial)
+    )((place % 2).reshape(1), far, centered, taper_sums, partial)
     return unpack(exchange(updated))
 
 

time: 133 us -> 133 us (level)
  no operation moved by 1% of the time
where the time goes in v5:
time: 133 us; the launch traced here: 132 us
  waiting for transfers between devices  57 us (43%)
  blocking collectives  46.8 us (35%)
  starting transfers between devices  18.2 us (14%)
  Pallas kernels  9.96 us (7%)
    all_to_all x1, waiting for transfers between devices, exchange(): lax.all_to_all(packed, 'mem', split_axis=0, concat_axis=0, tiled=True)  50.3 us
    all_to_all x1, blocking collectives, exchange(): lax.all_to_all(packed, 'mem', split_axis=0, concat_axis=0, tiled=True)  46.8 us
    all_to_all x1, starting transfers between devices, exchange(): lax.all_to_all(packed, 'mem', split_axis=0, concat_axis=0, tiled=True)  11.8 us
    ppermute x1, waiting for transfers between devices, on_device(): far = lax.ppermute(edges, 'mem', across)  5.8 us
  transfers between devices with their start and end apart: 4, of which 3 were waited for; matrix products, arithmetic and copies ran while one was open for 0% of the time, Pallas kernels for 3%

profile of v5, /device:TPU:1, one launch (start us, length us, event | category | flops | bytes accessed | tf_op | source)
XLA Modules:
  0.0 132.2 jit_solution(17729239393050469846)
XLA Ops:
  0.0 2.5 %shard_map.73 = bf16[64,4,16,256]{3,2,1,0:T(8,128)(2,1)} custom-call(bf16[3,16,16384]{2,1,0:T(8,128)(2,1)} %state.1, bf16[16,16384]{1,0:T(8,128)(2,1)} %noise.1), custom_call_target="tpu_custom_call" | custom-call | tf_op jit(solution)/shard_map/pallas_call | solution.py:170
  2.5 0.0 copy-start.4
  2.5 0.0 copy-start
  2.6 0.0 copy-start.2
  2.6 0.0 copy-start.1
  2.6 0.0 copy-start.3
  2.6 11.8 %all-to-all-start = ((bf16[64,4,16,256]{3,2,1,0:T(8,128)(2,1)}), bf16[64,4,16,256]{3,2,1,0:T(8,128)(2,1)S(1)}, u32[]{:S(2)}, u32[]{:S(2)}) async-start(bf16[64,4,16,256]{3,2,1,0:T(8,128)(2,1)} %shard_map.73), calls=%async_computation | async-start | bytes 4194304 | tf_op jit(solution)/shard_map/all_to_all | solution.py:218
  14.4 0.0 copy-done.4
  14.4 0.0 copy-done
  14.4 0.0 copy-done.2
  14.4 0.8 shard_map.74.tapers
  15.3 50.3 %all-to-all-done.arrived = bf16[64,4,16,256]{3,2,1,0:T(8,128)(2,1)S(1)} async-done(((bf16[64,4,16,256]{3,2,1,0:T(8,128)(2,1)}), bf16[64,4,16,256]{3,2,1,0:T(8,128)(2,1)S(1)}, u32[]{:S(2)}, u32[]{:S(2)}) %all-to-all-start) | async-done | bytes 2097184 | tf_op jit(solution)/shard_map/all_to_all | solution.py:218
  65.6 0.0 copy-done.1
  65.6 0.0 copy-done.3
  65.6 0.5 shard_map.75
  66.1 2.1 %collective-permute-start = (bf16[2,2,1024,128]{3,2,1,0:T(8,128)(2,1)S(1)}, bf16[2,2,1024,128]{3,2,1,0:T(8,128)(2,1)S(1)}, u32[]{:S(2)}, u32[]{:S(2)}) collective-permute-start(bf16[2,2,1024,128]{3,2,1,0:T(8,128)(2,1)S(1)} %get-tuple-element.8), channel_id=1, source_target_pairs={{8,16},{24,32},{40,48},{56,64},{72,80},{88,96},{104,112},{120,128}... | collective-permute-start | bytes 3145736 | tf_op jit(solution)/shard_map/ppermute | solution.py:245
  68.2 1.9 %collective-permute-start.1 = (bf16[2,1024,128]{2,1,0:T(8,128)(2,1)S(1)}, bf16[2,1024,128]{2,1,0:T(8,128)(2,1)S(1)}, u32[]{:S(2)}, u32[]{:S(2)}) collective-permute-start(bf16[2,1024,128]{2,1,0:T(8,128)(2,1)S(1)} %get-tuple-element.9.own), channel_id=1, source_target_pairs={{0,8},{8,0},{16,24},{24,16},{32,40},{40,32},{48,56},{56,48},{64,72... | collective-permute-start | bytes 1572872 | tf_op jit(solution)/shard_map/ppermute | solution.py:246
  70.1 2.4 %collective-permute-start.2 = (bf16[2,1024,128]{2,1,0:T(8,128)(2,1)S(1)}, bf16[2,1024,128]{2,1,0:T(8,128)(2,1)S(1)}, u32[]{:S(2)}, u32[]{:S(2)}) collective-permute-start(bf16[2,1024,128]{2,1,0:T(8,128)(2,1)S(1)} %get-tuple-element.10.own_weighted), channel_id=1, source_target_pairs={{0,8},{8,0},{16,24},{24,16},{32,40},{40,32},{48,56},{56,48},{64,72... | collective-permute-start | bytes 1572872 | tf_op jit(solution)/shard_map/ppermute | solution.py:247
  72.5 0.6 shard_map.76.centered
  73.2 0.0 collective-permute-done.1.mate
  73.2 0.9 collective-permute-done.2.mate_weighted
  74.1 2.4 %shard_map.77.partial = f32[2,1024,384]{2,1,0:T(8,128)S(1)} custom-call(bf16[2,1024,128]{2,1,0:T(8,128)(2,1)S(1)} %get-tuple-element.9.own, bf16[2,1024,128]{2,1,0:T(8,128)(2,1)S(1)} %collective-permute-done.1.mate, bf16[2,1024,128]{2,1,0:T(8,128)(2,1)S(1)} %get-tuple-element.10.own_weighted, bf16[2,1024,128]{2,1,0:T(8,128)(2,1)S(1)} %collective-permute-done.2.mate_weighted, ...), custom_call_target="tpu_custom_call" | custom-call | tf_op jit(solution)/shard_map/pallas_call | solution.py:255
  76.4 5.8 %collective-permute-done.across = bf16[2,2,1024,128]{3,2,1,0:T(8,128)(2,1)S(1)} collective-permute-done((bf16[2,2,1024,128]{3,2,1,0:T(8,128)(2,1)S(1)}, bf16[2,2,1024,128]{3,2,1,0:T(8,128)(2,1)S(1)}, u32[]{:S(2)}, u32[]{:S(2)}) %collective-permute-start) | collective-permute-done | bytes 1048608 | tf_op jit(solution)/shard_map/ppermute | solution.py:245
  82.2 1.9 %shard_map.78 = bf16[64,3,16,256]{3,2,1,0:T(8,128)(2,1)} custom-call(s32[1]{0:T(128)} %bitcast.core, bf16[2,2,1024,128]{3,2,1,0:T(8,128)(2,1)S(1)} %collective-permute-done.across, bf16[2,1024,384]{2,1,0:T(8,128)(2,1)S(1)} %shard_map.76.centered, f32[2,768,128]{2,1,0:T(8,128)S(1)} %shard_map.74.tapers, f32[2,1024,384]{2,1,0:T(8,128)S(1)} %shard_map.77.partial), custom_call_target="tpu_custom_call" | custom-call | tf_op jit(solution)/shard_map/pallas_call | solution.py:262
  84.2 46.8 %all_to_all.10.back = bf16[64,3,16,256]{3,2,1,0:T(8,128)(2,1)S(1)} all-to-all(bf16[64,3,16,256]{3,2,1,0:T(8,128)(2,1)} %shard_map.78), channel_id=1, replica_groups=mesh['mem'=64,'patch'=8] {'mem'}, dimensions={0} | all-to-all | bytes 3145728 | tf_op jit(solution)/shard_map/all_to_all | solution.py:218
  131.0 1.2 shard_map.79
  (1 shorter events, 0.0 us)
Async XLA Ops:
  2.5 11.9 %copy-start.4 = (s32[1,2,4]{2,1,0:T(2,128)S(1)}, s32[1,2,4]{2,1,0:T(2,128)}, u32[]{:S(2)}) copy-start(s32[1,2,4]{2,1,0:T(2,128)} %param.12) | copy-start | bytes 100
  2.5 11.9 %copy-start = (f32[8,128,128]{2,1,0:T(8,128)S(1)}, f32[8,128,128]{2,1,0:T(8,128)}, u32[]{:S(2)}) copy-start(f32[8,128,128]{2,1,0:T(8,128)} %table.1) | copy-start | bytes 1572868
  2.6 11.9 %copy-start.2 = (s32[1,2,4]{2,1,0:T(2,128)S(1)}, s32[1,2,4]{2,1,0:T(2,128)}, u32[]{:S(2)}) copy-start(s32[1,2,4]{2,1,0:T(2,128)} %param.13) | copy-start | bytes 100
  2.6 63.0 %copy-start.1 = (bf16[1,2,128,128]{3,2,1,0:T(8,128)(2,1)S(1)}, bf16[1,2,128,128]{3,2,1,0:T(8,128)(2,1)}, u32[]{:S(2)}) copy-start(bf16[1,2,128,128]{3,2,1,0:T(8,128)(2,1)} %param.10) | copy-start | bytes 196612
  2.6 63.0 %copy-start.3 = (f32[1,256]{1,0:T(1,128)S(1)}, f32[1,256]{1,0:T(1,128)}, u32[]{:S(2)}) copy-start(f32[1,256]{1,0:T(1,128)} %obs.1) | copy-start | bytes 3076
  2.6 63.0 %all-to-all-start = ((bf16[64,4,16,256]{3,2,1,0:T(8,128)(2,1)}), bf16[64,4,16,256]{3,2,1,0:T(8,128)(2,1)S(1)}, u32[]{:S(2)}, u32[]{:S(2)}) async-start(bf16[64,4,16,256]{3,2,1,0:T(8,128)(2,1)} %shard_map.73), calls=%async_computation | async-start | bytes 4194304 | tf_op jit(solution)/shard_map/all_to_all | solution.py:218
  66.1 16.1 %collective-permute-start = (bf16[2,2,1024,128]{3,2,1,0:T(8,128)(2,1)S(1)}, bf16[2,2,1024,128]{3,2,1,0:T(8,128)(2,1)S(1)}, u32[]{:S(2)}, u32[]{:S(2)}) collective-permute-start(bf16[2,2,1024,128]{3,2,1,0:T(8,128)(2,1)S(1)} %get-tuple-element.8), channel_id=1, source_target_pairs={{8,16},{24,32},{40,48},{56,64},{72,80},{88,96},{104,112},{120,128}... | collective-permute-start | bytes 3145736 | tf_op jit(solution)/shard_map/ppermute | solution.py:245
  68.2 5.0 %collective-permute-start.1 = (bf16[2,1024,128]{2,1,0:T(8,128)(2,1)S(1)}, bf16[2,1024,128]{2,1,0:T(8,128)(2,1)S(1)}, u32[]{:S(2)}, u32[]{:S(2)}) collective-permute-start(bf16[2,1024,128]{2,1,0:T(8,128)(2,1)S(1)} %get-tuple-element.9.own), channel_id=1, source_target_pairs={{0,8},{8,0},{16,24},{24,16},{32,40},{40,32},{48,56},{56,48},{64,72... | collective-permute-start | bytes 1572872 | tf_op jit(solution)/shard_map/ppermute | solution.py:246
  70.1 3.9 %collective-permute-start.2 = (bf16[2,1024,128]{2,1,0:T(8,128)(2,1)S(1)}, bf16[2,1024,128]{2,1,0:T(8,128)(2,1)S(1)}, u32[]{:S(2)}, u32[]{:S(2)}) collective-permute-start(bf16[2,1024,128]{2,1,0:T(8,128)(2,1)S(1)} %get-tuple-element.10.own_weighted), channel_id=1, source_target_pairs={{0,8},{8,0},{16,24},{24,16},{32,40},{40,32},{48,56},{56,48},{64,72... | collective-permute-start | bytes 1572872 | tf_op jit(solution)/shard_map/ppermute | solution.py:247

commit v6 on v5

--- a/solution.py
+++ b/solution.py
@@ -15,7 +15,7 @@
 LOCAL_MEMBERS = 16
 RING = 64
 TILES = MEMBERS // BLOCK
-PIECES = 4
+PIECES = 2
 
 VMEM = pl.BlockSpec(memory_space=pltpu.VMEM)
 SMEM = pl.BlockSpec(memory_space=pltpu.SMEM)
@@ -270,7 +270,8 @@
         ],
         compiler_params=PARAMS,
     )((place % 2).reshape(1), far, centered, taper_sums, partial)
-    return unpack(exchange(updated))
+    back = exchange(updated)
+    return jnp.transpose(back, (1, 2, 0, 3)).reshape(VARIABLES, LOCAL_MEMBERS, RING * CELLS)
 
 
 def solution(mesh):

time: 133 us -> 133 us (level)
  no operation moved by 1% of the time
where the time goes in v6:
time: 133 us; the launch traced here: 132 us
  waiting for transfers between devices  57 us (43%)
  blocking collectives  46.8 us (35%)
  starting transfers between devices  18.2 us (14%)
  Pallas kernels  8.95 us (7%)
    all_to_all x1, waiting for transfers between devices, exchange(): lax.all_to_all(packed, 'mem', split_axis=0, concat_axis=0, tiled=True)  50.3 us
    all_to_all x1, blocking collectives, exchange(): lax.all_to_all(packed, 'mem', split_axis=0, concat_axis=0, tiled=True)  46.8 us
    all_to_all x1, starting transfers between devices, exchange(): lax.all_to_all(packed, 'mem', split_axis=0, concat_axis=0, tiled=True)  11.8 us
    ppermute x1, waiting for transfers between devices, on_device(): far = lax.ppermute(edges, 'mem', across)  5.81 us
  transfers between devices with their start and end apart: 4, of which 3 were waited for; matrix products, arithmetic and copies ran while one was open for 0% of the time, Pallas kernels for 3%

profile of v6, /device:TPU:1, one launch (start us, length us, event | category | flops | bytes accessed | tf_op | source)
XLA Modules:
  0.0 132.4 jit_solution(11666806145030143121)
XLA Ops:
  0.0 2.6 %shard_map.73 = bf16[64,4,16,256]{3,2,1,0:T(8,128)(2,1)} custom-call(bf16[3,16,16384]{2,1,0:T(8,128)(2,1)} %state.1, bf16[16,16384]{1,0:T(8,128)(2,1)} %noise.1), custom_call_target="tpu_custom_call" | custom-call | tf_op jit(solution)/shard_map/pallas_call | solution.py:170
  2.6 0.0 copy-start.4
  2.7 0.0 copy-start
  2.7 0.0 copy-start.2
  2.7 0.0 copy-start.1
  2.7 0.0 copy-start.3
  2.7 11.8 %all-to-all-start = ((bf16[64,4,16,256]{3,2,1,0:T(8,128)(2,1)}), bf16[64,4,16,256]{3,2,1,0:T(8,128)(2,1)S(1)}, u32[]{:S(2)}, u32[]{:S(2)}) async-start(bf16[64,4,16,256]{3,2,1,0:T(8,128)(2,1)} %shard_map.73), calls=%async_computation | async-start | bytes 4194304 | tf_op jit(solution)/shard_map/all_to_all | solution.py:218
  14.5 0.0 copy-done.4
  14.5 0.0 copy-done
  14.5 0.0 copy-done.2
  14.5 0.8 shard_map.74.tapers
  15.4 50.3 %all-to-all-done.arrived = bf16[64,4,16,256]{3,2,1,0:T(8,128)(2,1)S(1)} async-done(((bf16[64,4,16,256]{3,2,1,0:T(8,128)(2,1)}), bf16[64,4,16,256]{3,2,1,0:T(8,128)(2,1)S(1)}, u32[]{:S(2)}, u32[]{:S(2)}) %all-to-all-start) | async-done | bytes 2097184 | tf_op jit(solution)/shard_map/all_to_all | solution.py:218
  65.7 0.0 copy-done.1
  65.7 0.0 copy-done.3
  65.7 0.5 shard_map.75
  66.2 2.1 %collective-permute-start = (bf16[2,2,1024,128]{3,2,1,0:T(8,128)(2,1)S(1)}, bf16[2,2,1024,128]{3,2,1,0:T(8,128)(2,1)S(1)}, u32[]{:S(2)}, u32[]{:S(2)}) collective-permute-start(bf16[2,2,1024,128]{3,2,1,0:T(8,128)(2,1)S(1)} %get-tuple-element.8), channel_id=1, source_target_pairs={{8,16},{24,32},{40,48},{56,64},{72,80},{88,96},{104,112},{120,128}... | collective-permute-start | bytes 3145736 | tf_op jit(solution)/shard_map/ppermute | solution.py:245
  68.3 1.9 %collective-permute-start.1 = (bf16[2,1024,128]{2,1,0:T(8,128)(2,1)S(1)}, bf16[2,1024,128]{2,1,0:T(8,128)(2,1)S(1)}, u32[]{:S(2)}, u32[]{:S(2)}) collective-permute-start(bf16[2,1024,128]{2,1,0:T(8,128)(2,1)S(1)} %get-tuple-element.9.own), channel_id=1, source_target_pairs={{0,8},{8,0},{16,24},{24,16},{32,40},{40,32},{48,56},{56,48},{64,72... | collective-permute-start | bytes 1572872 | tf_op jit(solution)/shard_map/ppermute | solution.py:246
  70.3 2.4 %collective-permute-start.2 = (bf16[2,1024,128]{2,1,0:T(8,128)(2,1)S(1)}, bf16[2,1024,128]{2,1,0:T(8,128)(2,1)S(1)}, u32[]{:S(2)}, u32[]{:S(2)}) collective-permute-start(bf16[2,1024,128]{2,1,0:T(8,128)(2,1)S(1)} %get-tuple-element.10.own_weighted), channel_id=1, source_target_pairs={{0,8},{8,0},{16,24},{24,16},{32,40},{40,32},{48,56},{56,48},{64,72... | collective-permute-start | bytes 1572872 | tf_op jit(solution)/shard_map/ppermute | solution.py:247
  72.7 0.6 shard_map.76.centered
  73.3 0.0 collective-permute-done.1.mate
  73.3 0.9 collective-permute-done.2.mate_weighted
  74.2 2.3 %shard_map.77.partial = f32[2,1024,384]{2,1,0:T(8,128)S(1)} custom-call(bf16[2,1024,128]{2,1,0:T(8,128)(2,1)S(1)} %get-tuple-element.9.own, bf16[2,1024,128]{2,1,0:T(8,128)(2,1)S(1)} %collective-permute-done.1.mate, bf16[2,1024,128]{2,1,0:T(8,128)(2,1)S(1)} %get-tuple-element.10.own_weighted, bf16[2,1024,128]{2,1,0:T(8,128)(2,1)S(1)} %collective-permute-done.2.mate_weighted, ...), custom_call_target="tpu_custom_call" | custom-call | tf_op jit(solution)/shard_map/pallas_call | solution.py:255
  76.5 5.8 %collective-permute-done.across = bf16[2,2,1024,128]{3,2,1,0:T(8,128)(2,1)S(1)} collective-permute-done((bf16[2,2,1024,128]{3,2,1,0:T(8,128)(2,1)S(1)}, bf16[2,2,1024,128]{3,2,1,0:T(8,128)(2,1)S(1)}, u32[]{:S(2)}, u32[]{:S(2)}) %collective-permute-start) | collective-permute-done | bytes 1048608 | tf_op jit(solution)/shard_map/ppermute | solution.py:245
  82.3 2.0 %shard_map.78 = bf16[64,3,16,256]{3,2,1,0:T(8,128)(2,1)} custom-call(s32[1]{0:T(128)} %bitcast.core, bf16[2,2,1024,128]{3,2,1,0:T(8,128)(2,1)S(1)} %collective-permute-done.across, bf16[2,1024,384]{2,1,0:T(8,128)(2,1)S(1)} %shard_map.76.centered, f32[2,768,128]{2,1,0:T(8,128)S(1)} %shard_map.74.tapers, f32[2,1024,384]{2,1,0:T(8,128)S(1)} %shard_map.77.partial), custom_call_target="tpu_custom_call" | custom-call | tf_op jit(solution)/shard_map/pallas_call | solution.py:262
  84.3 46.8 %all_to_all.10 = bf16[64,3,16,256]{3,2,1,0:T(8,128)(2,1)S(1)} all-to-all(bf16[64,3,16,256]{3,2,1,0:T(8,128)(2,1)} %shard_map.78), channel_id=1, replica_groups=mesh['mem'=64,'patch'=8] {'mem'}, dimensions={0} | all-to-all | bytes 3145728 | tf_op jit(solution)/shard_map/all_to_all | solution.py:218
  131.2 1.2 copy.9
  (1 shorter events, 0.0 us)
Async XLA Ops:
  2.6 11.9 %copy-start.4 = (s32[1,2,4]{2,1,0:T(2,128)S(1)}, s32[1,2,4]{2,1,0:T(2,128)}, u32[]{:S(2)}) copy-start(s32[1,2,4]{2,1,0:T(2,128)} %param.12) | copy-start | bytes 100
  2.7 11.9 %copy-start = (f32[8,128,128]{2,1,0:T(8,128)S(1)}, f32[8,128,128]{2,1,0:T(8,128)}, u32[]{:S(2)}) copy-start(f32[8,128,128]{2,1,0:T(8,128)} %table.1) | copy-start | bytes 1572868
  2.7 11.9 %copy-start.2 = (s32[1,2,4]{2,1,0:T(2,128)S(1)}, s32[1,2,4]{2,1,0:T(2,128)}, u32[]{:S(2)}) copy-start(s32[1,2,4]{2,1,0:T(2,128)} %param.13) | copy-start | bytes 100
  2.7 63.0 %copy-start.1 = (bf16[1,2,128,128]{3,2,1,0:T(8,128)(2,1)S(1)}, bf16[1,2,128,128]{3,2,1,0:T(8,128)(2,1)}, u32[]{:S(2)}) copy-start(bf16[1,2,128,128]{3,2,1,0:T(8,128)(2,1)} %param.10) | copy-start | bytes 196612
  2.7 63.0 %copy-start.3 = (f32[1,256]{1,0:T(1,128)S(1)}, f32[1,256]{1,0:T(1,128)}, u32[]{:S(2)}) copy-start(f32[1,256]{1,0:T(1,128)} %obs.1) | copy-start | bytes 3076
  2.7 63.0 %all-to-all-start = ((bf16[64,4,16,256]{3,2,1,0:T(8,128)(2,1)}), bf16[64,4,16,256]{3,2,1,0:T(8,128)(2,1)S(1)}, u32[]{:S(2)}, u32[]{:S(2)}) async-start(bf16[64,4,16,256]{3,2,1,0:T(8,128)(2,1)} %shard_map.73), calls=%async_computation | async-start | bytes 4194304 | tf_op jit(solution)/shard_map/all_to_all | solution.py:218
  66.2 16.1 %collective-permute-start = (bf16[2,2,1024,128]{3,2,1,0:T(8,128)(2,1)S(1)}, bf16[2,2,1024,128]{3,2,1,0:T(8,128)(2,1)S(1)}, u32[]{:S(2)}, u32[]{:S(2)}) collective-permute-start(bf16[2,2,1024,128]{3,2,1,0:T(8,128)(2,1)S(1)} %get-tuple-element.8), channel_id=1, source_target_pairs={{8,16},{24,32},{40,48},{56,64},{72,80},{88,96},{104,112},{120,128}... | collective-permute-start | bytes 3145736 | tf_op jit(solution)/shard_map/ppermute | solution.py:245
  68.3 5.0 %collective-permute-start.1 = (bf16[2,1024,128]{2,1,0:T(8,128)(2,1)S(1)}, bf16[2,1024,128]{2,1,0:T(8,128)(2,1)S(1)}, u32[]{:S(2)}, u32[]{:S(2)}) collective-permute-start(bf16[2,1024,128]{2,1,0:T(8,128)(2,1)S(1)} %get-tuple-element.9.own), channel_id=1, source_target_pairs={{0,8},{8,0},{16,24},{24,16},{32,40},{40,32},{48,56},{56,48},{64,72... | collective-permute-start | bytes 1572872 | tf_op jit(solution)/shard_map/ppermute | solution.py:246
  70.3 3.9 %collective-permute-start.2 = (bf16[2,1024,128]{2,1,0:T(8,128)(2,1)S(1)}, bf16[2,1024,128]{2,1,0:T(8,128)(2,1)S(1)}, u32[]{:S(2)}, u32[]{:S(2)}) collective-permute-start(bf16[2,1024,128]{2,1,0:T(8,128)(2,1)S(1)} %get-tuple-element.10.own_weighted), channel_id=1, source_target_pairs={{0,8},{8,0},{16,24},{24,16},{32,40},{40,32},{48,56},{56,48},{64,72... | collective-permute-start | bytes 1572872 | tf_op jit(solution)/shard_map/ppermute | solution.py:247
